TPU v7x, 256 devices: a whole 4x4x8 slice. The times are simulated.
256 devices in a mesh: dp: 16 (over x, y_lo, core), prec: 8 (over z), pair: 2 (over y_hi).
Axes of the slice: x: 4, y: 4 (y_hi: 2, y_lo: 2; y = y_hi * 2 + y_lo), z: 8, core: 2. Of those that a mesh axis runs over, the one named last changes fastest.
Arguments:
- activations: bfloat16 [4096, 4096], P('dp', 'prec')
- output_grads: bfloat16 [4096, 16384], P('dp', 'pair')
- iter_counts: int32 [32, 8], P(('pair', 'dp'), 'prec'), may hold values from 1 to 2, as said below
Outputs:
- preconditioned: float32 [16384, 4096], P(('pair', 'dp'), 'prec')
Inputs may be any that keep to these rules, and one draw needn't show every extreme that they name: `iter_counts`: newton iterations of each block; 2 is taken by at least one block in every draw.
All inputs are finite; a program needn't handle non-finite values.
Results may differ from a plain program's by a relative error of at most 0.0003.
Values may be sent and summed in bfloat16 or wider, within the bound.
No kernel may reach another device: no remote copies, remote signals or barrier semaphores. Data moves between devices by JAX's collectives and lax.ppermute only.
A program may use at most 64 MiB of HBM per device.

v0:
```python
import jax
import jax.numpy as jnp
from jax import lax
from jax.sharding import PartitionSpec as P

BLK = 512


SHIFT = 0.001


def product(left, right):
    return jnp.dot(left, right, precision=lax.Precision.HIGHEST)


def inverse_root(statistic, plan):
    extent = statistic.shape[0]
    identity = jnp.eye(extent, dtype=statistic.dtype)
    shifted = statistic + SHIFT * identity
    scaling = 2.5 / jnp.sqrt(jnp.sum(shifted * shifted) + 1e-06)
    inverse = identity * jnp.sqrt(jnp.sqrt(scaling))
    coupled = shifted * scaling

    def advance(step_index, state_pair):
        current, matrix = state_pair
        factor = 1.25 * identity - 0.25 * matrix
        square = product(factor, factor)
        return (product(current, factor), product(product(square, square), matrix))

    inverse, coupled = lax.fori_loop(0, plan, advance, (inverse, coupled))
    return inverse


def both_roots(item):
    block, plan = item
    left_root = inverse_root(product(block, block.T), plan)
    right_root = inverse_root(product(block.T, block), plan)
    return (left_root, right_root)


def per_device(activations, output_grads, iter_counts):
    dp_size = lax.axis_size("dp")
    row_count = output_grads.shape[1] // dp_size
    feature_count = activations.shape[1]
    contract = (((0,), (0,)), ((), ()))
    grad_block = lax.psum_scatter(
        lax.dot_general(output_grads, activations, contract, preferred_element_type=jnp.float32),
        "dp",
        scatter_dimension=0,
        tiled=True,
    )
    ff_blocks = row_count // BLK
    d_blocks = feature_count // BLK
    blocks = (
        grad_block.reshape(ff_blocks, BLK, d_blocks, BLK)
        .transpose(0, 2, 1, 3)
        .reshape(ff_blocks * d_blocks, BLK, BLK)
    )
    plan = iter_counts.reshape(-1)
    left_roots, right_roots = lax.map(both_roots, (blocks, plan))
    highest = lax.Precision.HIGHEST
    updates = jnp.einsum(
        "bij,bjk->bik",
        jnp.einsum("bij,bjk->bik", left_roots, blocks, precision=highest),
        right_roots,
        precision=highest,
    )
    grad_squares, update_squares = lax.psum(
        (jnp.sum(blocks * blocks), jnp.sum(updates * updates)), ("dp", "prec", "pair")
    )
    graft_ratio = jnp.sqrt(grad_squares / update_squares)
    scaled = updates * graft_ratio
    return (
        scaled.reshape(ff_blocks, d_blocks, BLK, BLK)
        .transpose(0, 2, 1, 3)
        .reshape(row_count, feature_count)
    )


def solution(mesh):
    in_specs = (P("dp", "prec"), P("dp", "pair"), P(("pair", "dp"), "prec"))
    out_specs = P(("pair", "dp"), "prec")
    return jax.shard_map(
        per_device, mesh=mesh, in_specs=in_specs, out_specs=out_specs, check_vma=False
    )
```

profile of v0, /device:TPU:1, one launch (start us, length us, event | category | flops | bytes accessed | tf_op | source)
XLA Modules:
  0.0 346.3 jit_solution(13254080549746700504)
XLA Ops:
  6.5 0.0 copy-start
  6.5 0.0 reduce-scatter.2.cloned.1.call-start
  6.5 0.9 copy-done
  7.5 10.3 %fusion.36 = f32[8192,512]{1,0:T(8,128)} fusion(bf16[256,8192]{1,0:T(8,128)(2,1)} %param.8, bf16[256,512]{1,0:T(8,128)(2,1)S(1)} %copy-done), kind=kOutput, calls=%fused_computation.50 | convolution fusion | flops 2147483648 | bytes 21233664 | tf_op jit(solution)/shard_map/dot_general | solution.py:47
  17.8 0.0 reduce-scatter.2.cloned.1.call-update
  17.8 187.3 %reduce-scatter.2.cloned.1.call-done = f32[512,512]{1,0:T(8,128)} async-done(((f32[8192,512]{1,0:T(8,128)}), f32[512,512]{1,0:T(8,128)}) %reduce-scatter.2.cloned.1.call-update) | async-done | bytes 1048592 | tf_op jit(solution)/shard_map/reduce_scatter | solution.py:46
  205.1 4.3 %multiply_reduce_fusion.3 = (f32[]{:T(128)}, f32[512,512]{1,0:T(8,128)S(1)}) fusion(f32[512,512]{1,0:T(8,128)} %reduce-scatter.2.cloned.1.call-done), kind=kOutput, calls=%fused_computation.39 | convolution fusion | flops 1611923456 | bytes 2097156 | tf_op jit(solution)/shard_map/while/body/eval_jaxpr/dot_general | solution.py:13
  210.1 0.1 broadcast_multiply_fusion.2
  210.3 0.1 fusion.31
  210.4 0.3 copy.4
  210.7 0.0 copy-start.1
  210.8 9.3 %while.37 = (s32[]{:T(128)}, f32[512,512]{0,1:T(8,128)S(1)}, f32[512,512]{1,0:T(8,128)S(1)}, s32[]{:T(128)}, s32[]{:T(128)}) while((s32[]{:T(128)}, f32[512,512]{0,1:T(8,128)S(1)}, f32[512,512]{1,0:T(8,128)S(1)}, s32[]{:T(128)}, s32[]{:T(128)}) %tuple.44), condition=%wide.region_3.4_spmd.clone, body=%wide.region_2.3_spmd.clone.sunk | while | flops 6444548096 | bytes 14680125 | solution.py:30
  211.7 0.1 copy.30
  211.8 0.1 copy.29
  211.8 1.9 convolution_bitcast_fusion.4
  213.8 1.9 fusion.79
  215.7 1.8 fusion.80
  217.5 1.8 fusion.81
  220.0 0.0 copy-done.1
  220.1 2.6 multiply_reduce_fusion.2
  223.4 1.1 broadcast_multiply_fusion.1
  224.5 1.1 fusion.30
  225.6 1.6 copy.5
  227.2 11.4 %while.38 = (s32[]{:T(128)}, f32[512,512]{0,1:T(8,128)S(1)}, f32[512,512]{1,0:T(8,128)}, s32[]{:T(128)}, s32[]{:T(128)}) while((s32[]{:T(128)}, f32[512,512]{0,1:T(8,128)S(1)}, f32[512,512]{1,0:T(8,128)}, s32[]{:T(128)}, s32[]{:T(128)}) %tuple.47), condition=%wide.region_6.7_spmd.clone, body=%wide.region_5.6_spmd.clone.sunk | while | flops 6444548096 | bytes 14680125 | solution.py:30
  228.0 1.2 copy.32
  229.3 0.1 copy.31
  229.3 1.9 convolution_bitcast_fusion.5
  231.2 1.9 fusion.87
  233.2 1.8 fusion.88
  235.0 2.8 fusion.89
  238.5 1.8 fusion.37
  240.4 2.6 multiply_reduce_fusion
  243.0 0.9 multiply_reduce_fusion.1
  243.9 93.0 %all-reduce = (f32[]{:T(128)}, f32[]{:T(128)}) all-reduce(f32[]{:T(128)} %multiply_reduce_fusion.1, f32[]{:T(128)} %get-tuple-element.130), channel_id=1, replica_groups=mesh['dp'=16,'prec'=8,'pair'=2] {'dp','prec','pair'}, use_global_device_ids=true, to_apply=%region_8.9 | all-reduce | flops 2 | bytes 16 | tf_op jit(solution)/shard_map/psum | solution.py:68
  338.3 1.1 broadcast_multiply_fusion
Async XLA Ops:
  6.5 1.0 copy-start
  6.5 198.5 %reduce-scatter.2.cloned.1.call-start = ((), (), s32[]{:S(2)}) async-start(), calls=%async_computation.1 | async-start | bytes 17825792 | tf_op jit(solution)/shard_map/reduce_scatter | solution.py:46
  210.7 9.3 %copy-start.1 = (f32[512,512]{1,0:T(8,128)S(1)}, f32[512,512]{1,0:T(8,128)}, u32[]{:S(2)}) copy-start(f32[512,512]{1,0:T(8,128)} %reduce-scatter.2.cloned.1.call-done) | copy-start | bytes 3145732
Sparse Core Ops, SparseCore 0:
  17.9 187.1 reduce-scatter.1
where the time goes:
time: 347 us; the launch traced here: 346 us
  waiting for transfers between devices  187 us (54%)
  blocking collectives  93 us (27%)
  matrix products  37.6 us (11%)
  between operations  16.5 us (5%)
  other arithmetic  4.38 us (1%)
  local copies, waits for them, and re-layouts  4.27 us (1%)
    reduce_scatter x1, waiting for transfers between devices, per_device(): lax.psum_scatter(lax.dot_general(output_grads, activations, contract, pre...  187 us
    psum x1, blocking collectives, per_device(): lax.psum((jnp.sum(blocks * blocks), jnp.sum(updates * updates)), ('dp', '...  93 us
    dot_general x10, matrix products, product(): return jnp.dot(left, right, precision=lax.Precision.HIGHEST)  22.9 us
    dot_general x1, matrix products, per_device(): lax.dot_general(output_grads, activations, contract, preferred_element_ty...  10.3 us
  transfers between devices with their start and end apart: 1, of which 1 were waited for; matrix products, arithmetic and copies ran while one was open for 0% of the time, Pallas kernels for 0%

commit v1 on v0

v1 whole, which is shorter than its diff:
```python
import jax
import jax.numpy as jnp
from jax import lax
from jax.experimental import pallas as pl
from jax.experimental.pallas import tpu as pltpu
from jax.sharding import Mesh, PartitionSpec as P

BLK = 512
SHIFT = 0.001
DP = ("x", "yl", "core")
EVERY = ("x", "yl", "core", "prec", "pair")
ROWS_BY_ROWS = (((1,), (1,)), ((), ()))
ROWS_BY_COLUMNS = (((1,), (0,)), ((), ()))


def dot(left, right, contract=ROWS_BY_COLUMNS):
    return lax.dot_general(left, right, contract, preferred_element_type=jnp.float32)


def split(matrix):
    high = matrix.astype(jnp.bfloat16)
    return high, (matrix - high.astype(jnp.float32)).astype(jnp.bfloat16)


def product(left, right, contract=ROWS_BY_COLUMNS):
    (left_high, left_low), (right_high, right_low) = left, right
    return dot(left_high, right_high, contract) + (
        dot(left_high, right_low, contract) + dot(left_low, right_high, contract)
    )


def block_step(place_ref, grads_ref, near_ref, far_ref, update_ref, sums_ref, grad_ref, root_ref):
    shard = place_ref[0, 1]
    total = None
    for part in range(16):
        across, step = part // 8, part % 8
        offset = (step % 4) * 4 + (step // 4) * 2 + across
        acts_ref = far_ref if across else near_ref
        term = dot(acts_ref[step], grads_ref[shard ^ offset])
        total = term if total is None else total + term
    grad_ref[...] = total
    grad = grad_ref[...]
    grad_parts = split(grad)
    statistic = product(grad_parts, grad_parts, ROWS_BY_ROWS)
    on_diagonal = lax.broadcasted_iota(jnp.int32, (BLK, BLK), 0) == lax.broadcasted_iota(
        jnp.int32, (BLK, BLK), 1
    )
    shifted = statistic + jnp.where(on_diagonal, jnp.float32(SHIFT), jnp.float32(0.0))
    scaling = 2.5 / jnp.sqrt(jnp.sum(shifted * shifted) + 1e-06)
    root_ref[...] = jnp.where(on_diagonal, jnp.float32(1.25), jnp.float32(0.0)) - (
        0.25 * scaling
    ) * shifted

    @pl.when(place_ref[0, 0] == 2)
    def _():
        factor = root_ref[...]
        factor_parts = split(factor)
        square = product(factor_parts, factor_parts)
        square_parts = split(square)
        fourth = product(square_parts, square_parts)
        root_ref[...] = 1.25 * factor + product(split(fourth), split(square - 1.25 * factor))

    root_parts = split(root_ref[...])
    half = product(root_parts, grad_parts)
    update = product(root_parts, split(half)) * jnp.sqrt(scaling)
    update_ref[...] = update.T
    lane = lax.broadcasted_iota(jnp.int32, (8, 128), 1)
    grad_squares = jnp.sum(grad * grad)
    update_squares = jnp.sum(update * update)
    sums_ref[...] = jnp.where(lane == 0, grad_squares, jnp.where(lane == 1, update_squares, 0.0))


def run_block(place, grads, near, far):
    vmem = pl.BlockSpec(memory_space=pltpu.VMEM)
    return pl.pallas_call(
        block_step,
        out_shape=(
            jax.ShapeDtypeStruct((BLK, BLK), jnp.float32),
            jax.ShapeDtypeStruct((8, 128), jnp.float32),
        ),
        in_specs=[pl.BlockSpec(memory_space=pltpu.SMEM), vmem, vmem, vmem],
        out_specs=(vmem, vmem),
        scratch_shapes=[pltpu.VMEM((BLK, BLK), jnp.float32)] * 2,
        compiler_params=pltpu.CompilerParams(vmem_limit_bytes=48 << 20),
    )(place, grads, near, far)


def swap(value, axes, bits):
    size = 1
    for axis in axes:
        size *= lax.axis_size(axis)
    return lax.ppermute(value, axes, [(i, i ^ bits) for i in range(size)])


def per_device(activations, output_grads, iter_counts):
    tokens = output_grads.shape[0]
    shards = 16
    pieces = output_grads.reshape(tokens, shards, BLK).transpose(1, 0, 2)
    grads = lax.all_to_all(pieces, DP, 0, 0, tiled=True)

    own = activations.T
    along_x = jnp.stack([own] + [swap(own, ("x",), bits) for bits in (1, 2, 3)])
    near = jnp.concatenate([along_x, swap(along_x, ("yl", "pair"), 3)])
    far = swap(near, ("core",), 1)

    place = jnp.stack([iter_counts[0, 0], lax.axis_index(DP)]).reshape(1, 2).astype(jnp.int32)
    update, sums = run_block(place, grads, near, far)

    shared = jnp.broadcast_to(sums[None, :1], (256, 1, 128))
    gathered = lax.all_to_all(shared, EVERY, 0, 0, tiled=True)
    totals = jnp.sum(gathered, axis=(0, 1))
    return update * jnp.sqrt(totals[0] / totals[1])


def solution(mesh):
    fine = Mesh(mesh.devices.reshape(4, 2, 2, 8, 2), EVERY)
    in_specs = (P(DP, "prec"), P(DP, "pair"), P(("pair",) + DP, "prec"))
    out_specs = P(("pair",) + DP, "prec")
    return jax.shard_map(
        per_device, mesh=fine, in_specs=in_specs, out_specs=out_specs, check_vma=False
    )
```

time: 347 us -> 159 us (0.46)
  waiting for transfers between devices: 187 us -> 92.8 us
  blocking collectives: 93 us -> 26 us
  matrix products: 37.6 us -> 0 us
  between operations: 16.5 us -> 2.03 us
  starting transfers between devices: 0.01 us -> 13.6 us
  local copies, waits for them, and re-layouts: 4.27 us -> 13.8 us
  Pallas kernels: 0 us -> 8.77 us
    reduce_scatter x1 -> x0, waiting for transfers between devices: 187 us -> none  [per_device(): lax.psum_scatter(lax.dot_general(output_grads, activations, contract, pre...]
    psum x1 -> x0, blocking collectives: 93 us -> none  [per_device(): lax.psum((jnp.sum(blocks * blocks), jnp.sum(updates * updates)), ('dp', '...]
    ppermute x0 -> x5, waiting for transfers between devices: none -> 92.8 us  [swap(): return lax.ppermute(value, axes, [(i, i ^ bits) for i in range(size)])]
    dot_general x13 -> x0, matrix products: 37.6 us -> none  [the longest x10 22.9 us: product(): return jnp.dot(left, right, precision=lax.Precision.HIGHEST)]
    all_to_all x0 -> x1, blocking collectives: none -> 26 us  [per_device(): gathered = lax.all_to_all(shared, EVERY, 0, 0, tiled=True)]
    pallas_call x0 -> x1, Pallas kernels: none -> 8.77 us  [run_block(): pl.pallas_call(block_step, out_shape=(jax.ShapeDtypeStruct((BLK, BLK), jn...]
    all_to_all x0 -> x1, starting transfers between devices: none -> 7.64 us  [per_device(): grads = lax.all_to_all(pieces, DP, 0, 0, tiled=True)]
    reshape x0 -> x1, local copies, waits for them, and re-layouts: none -> 6.39 us  [per_device(): pieces = output_grads.reshape(tokens, shards, BLK).transpose(1, 0, 2)]
  transfers between devices with their start and end apart: 1 -> 6, of which waited for: 1 -> 4; matrix products, arithmetic and copies ran while one was open for 0% -> 0% of each run, Pallas kernels for 0% -> 0%
where the time goes in v1:
time: 159 us; the launch traced here: 158 us
  waiting for transfers between devices  92.8 us (58%)
  blocking collectives  26 us (16%)
  local copies, waits for them, and re-layouts  13.8 us (9%)
  starting transfers between devices  13.6 us (9%)
  Pallas kernels  8.77 us (6%)
  between operations  2.03 us (1%)
    ppermute x5, waiting for transfers between devices, swap(): return lax.ppermute(value, axes, [(i, i ^ bits) for i in range(size)])  92.8 us
    all_to_all x1, blocking collectives, per_device(): gathered = lax.all_to_all(shared, EVERY, 0, 0, tiled=True)  26 us
    pallas_call x1, Pallas kernels, run_block(): pl.pallas_call(block_step, out_shape=(jax.ShapeDtypeStruct((BLK, BLK), jn...  8.77 us
    all_to_all x1, starting transfers between devices, per_device(): grads = lax.all_to_all(pieces, DP, 0, 0, tiled=True)  7.64 us
    unnamed x8, local copies, waits for them, and re-layouts  6.63 us
    reshape x1, local copies, waits for them, and re-layouts, per_device(): pieces = output_grads.reshape(tokens, shards, BLK).transpose(1, 0, 2)  6.39 us
    ppermute x5, starting transfers between devices, swap(): return lax.ppermute(value, axes, [(i, i ^ bits) for i in range(size)])  5.94 us
  transfers between devices with their start and end apart: 6, of which 4 were waited for; matrix products, arithmetic and copies ran while one was open for 0% of the time, Pallas kernels for 0%

profile of v1, /device:TPU:1, one launch (start us, length us, event | category | flops | bytes accessed | tf_op | source)
XLA Modules:
  0.0 158.2 jit_solution(16611325517777820655)
XLA Ops:
  0.0 6.4 %copy.11 = bf16[256,8192]{0,1:T(8,128)(2,1)} copy(bf16[256,8192]{1,0:T(8,128)(2,1)} %param.4) | data formatting | bytes 8388608 | tf_op args[1]
  6.4 6.4 %copy.12 = bf16[256,16,512]{2,0,1:T(8,128)(2,1)} copy(bf16[256,16,512]{0,2,1:T(8,128)(2,1)} %bitcast.22) | data formatting | bytes 8388608 | tf_op jit(solution)/shard_map/reshape | solution.py:98
  12.8 0.0 copy-start
  12.8 7.6 %all-to-all-start = ((bf16[16,256,512]{2,1,0:T(8,128)(2,1)}), bf16[16,256,512]{2,1,0:T(8,128)(2,1)}, u32[]{:S(2)}, u32[]{:S(2)}) async-start(bf16[16,256,512]{2,1,0:T(8,128)(2,1)} %bitcast.21), calls=%async_computation | async-start | bytes 8388608 | tf_op jit(solution)/shard_map/all_to_all | solution.py:99
  20.5 0.0 copy-done
  20.5 0.1 copy.13
  20.6 1.5 collective-permute-start
  22.1 2.4 %collective-permute-start.1 = (bf16[512,256]{1,0:T(8,128)(2,1)S(1)}, bf16[512,256]{1,0:T(8,128)(2,1)S(1)}, u32[]{:S(2)}, u32[]{:S(2)}) collective-permute-start(bf16[512,256]{1,0:T(8,128)(2,1)S(1)} %bitcast.24), channel_id=1, source_target_pairs={{0,128},{64,192},{128,0},{192,64},{1,129},{65,193},{129,1},{193,65... | collective-permute-start | bytes 786440 | tf_op jit(solution)/shard_map/ppermute | solution.py:92
  24.5 0.0 collective-permute-start.2
  24.6 52.8 %collective-permute-done = bf16[512,256]{1,0:T(8,128)(2,1)S(1)} collective-permute-done((bf16[512,256]{1,0:T(8,128)(2,1)S(1)}, bf16[512,256]{1,0:T(8,128)(2,1)S(1)}, u32[]{:S(2)}, u32[]{:S(2)}) %collective-permute-start) | collective-permute-done | bytes 262176 | tf_op jit(solution)/shard_map/ppermute | solution.py:92
  77.4 11.9 %collective-permute-done.1 = bf16[512,256]{1,0:T(8,128)(2,1)S(1)} collective-permute-done((bf16[512,256]{1,0:T(8,128)(2,1)S(1)}, bf16[512,256]{1,0:T(8,128)(2,1)S(1)}, u32[]{:S(2)}, u32[]{:S(2)}) %collective-permute-start.1) | collective-permute-done | bytes 262176 | tf_op jit(solution)/shard_map/ppermute | solution.py:92
  89.3 0.0 collective-permute-done.2
  89.3 0.1 pad_maximum_fusion
  89.4 0.1 collective-permute-start.3
  89.7 24.9 %collective-permute-done.3 = bf16[4,512,256]{2,1,0:T(8,128)(2,1)S(1)} collective-permute-done((bf16[4,512,256]{2,1,0:T(8,128)(2,1)S(1)}, bf16[4,512,256]{2,1,0:T(8,128)(2,1)S(1)}, u32[]{:S(2)}, u32[]{:S(2)}) %collective-permute-start.3) | collective-permute-done | bytes 1048608 | tf_op jit(solution)/shard_map/ppermute | solution.py:92
  114.5 0.1 constant_dynamic-update-slice_fusion.near_ref
  114.6 1.9 %collective-permute-start.4 = (bf16[8,512,256]{2,1,0:T(8,128)(2,1)S(1)}, bf16[8,512,256]{2,1,0:T(8,128)(2,1)}, u32[]{:S(2)}, u32[]{:S(2)}) collective-permute-start(bf16[8,512,256]{2,1,0:T(8,128)(2,1)S(1)} %constant_dynamic-update-slice_fusion.near_ref), channel_id=1, source_target_pairs={{0,16},{16,0},{1,17},{17,1},{2,18},{18,2},{3,19},{19,3},{4,20},{20... | collective-permute-start | bytes 6291464 | tf_op jit(solution)/shard_map/ppermute | solution.py:92
  117.1 0.1 add_bitcast_fusion.place_ref
  117.2 3.2 %collective-permute-done.4.far_ref = bf16[8,512,256]{2,1,0:T(8,128)(2,1)} collective-permute-done((bf16[8,512,256]{2,1,0:T(8,128)(2,1)S(1)}, bf16[8,512,256]{2,1,0:T(8,128)(2,1)}, u32[]{:S(2)}, u32[]{:S(2)}) %collective-permute-start.4) | collective-permute-done | bytes 2097184 | tf_op jit(solution)/shard_map/ppermute | solution.py:92
  120.4 0.0 all-to-all-done.grads_ref
  120.4 8.8 %shard_map.37 = (f32[512,512]{1,0:T(8,128)S(1)}, f32[8,128]{1,0:T(8,128)S(1)}) custom-call(s32[1,2]{1,0:T(1,128)S(1)} %add_bitcast_fusion.place_ref, bf16[16,256,512]{2,1,0:T(8,128)(2,1)} %all-to-all-done.grads_ref, bf16[8,512,256]{2,1,0:T(8,128)(2,1)S(1)} %constant_dynamic-update-slice_fusion.near_ref, bf16[8,512,256]{2,1,0:T(8,128)(2,1)} %collective-permute-done.4.far_ref), custom_call_target="tpu_custom_call" | custom-call | tf_op jit(solution)/shard_map/pallas_call | solution.py:75
  129.2 0.1 broadcast_in_dim.9
  129.3 26.0 %all_to_all.10 = f32[256,1,128]{2,1,0:T(1,128)S(1)} all-to-all(f32[256,1,128]{2,1,0:T(1,128)S(1)} %broadcast_in_dim.9), channel_id=1, replica_groups=mesh['x'=4,'yl'=2,'core'=2,'prec'=8,'pair'=2] {'x','yl','core','prec','p..., dimensions={0} | all-to-all | bytes 262144 | tf_op jit(solution)/shard_map/all_to_all | solution.py:110
  155.3 0.6 fusion
  157.2 1.1 broadcast_multiply_fusion
  (6 shorter events, 0.1 us)
Async XLA Ops:
  12.8 7.6 %copy-start = (bf16[256,512]{1,0:T(8,128)(2,1)S(1)}, bf16[256,512]{1,0:T(8,128)(2,1)}, u32[]{:S(2)}) copy-start(bf16[256,512]{1,0:T(8,128)(2,1)} %param.3) | copy-start | bytes 786436
  12.8 107.6 %all-to-all-start = ((bf16[16,256,512]{2,1,0:T(8,128)(2,1)}), bf16[16,256,512]{2,1,0:T(8,128)(2,1)}, u32[]{:S(2)}, u32[]{:S(2)}) async-start(bf16[16,256,512]{2,1,0:T(8,128)(2,1)} %bitcast.21), calls=%async_computation | async-start | bytes 8388608 | tf_op jit(solution)/shard_map/all_to_all | solution.py:99
  20.6 56.8 %collective-permute-start = (bf16[512,256]{1,0:T(8,128)(2,1)S(1)}, bf16[512,256]{1,0:T(8,128)(2,1)S(1)}, u32[]{:S(2)}, u32[]{:S(2)}) collective-permute-start(bf16[512,256]{1,0:T(8,128)(2,1)S(1)} %bitcast.23), channel_id=1, source_target_pairs={{0,64},{64,0},{128,192},{192,128},{1,65},{65,1},{129,193},{193,129... | collective-permute-start | bytes 786440 | tf_op jit(solution)/shard_map/ppermute | solution.py:92
  22.1 67.2 %collective-permute-start.1 = (bf16[512,256]{1,0:T(8,128)(2,1)S(1)}, bf16[512,256]{1,0:T(8,128)(2,1)S(1)}, u32[]{:S(2)}, u32[]{:S(2)}) collective-permute-start(bf16[512,256]{1,0:T(8,128)(2,1)S(1)} %bitcast.24), channel_id=1, source_target_pairs={{0,128},{64,192},{128,0},{192,64},{1,129},{65,193},{129,1},{193,65... | collective-permute-start | bytes 786440 | tf_op jit(solution)/shard_map/ppermute | solution.py:92
  24.5 64.8 %collective-permute-start.2 = (bf16[512,256]{1,0:T(8,128)(2,1)S(1)}, bf16[512,256]{1,0:T(8,128)(2,1)S(1)}, u32[]{:S(2)}, u32[]{:S(2)}) collective-permute-start(bf16[512,256]{1,0:T(8,128)(2,1)S(1)} %bitcast.25), channel_id=1, source_target_pairs={{0,192},{64,128},{128,64},{192,0},{1,193},{65,129},{129,65},{193,1... | collective-permute-start | bytes 786440 | tf_op jit(solution)/shard_map/ppermute | solution.py:92
  89.4 25.1 %collective-permute-start.3 = (bf16[4,512,256]{2,1,0:T(8,128)(2,1)S(1)}, bf16[4,512,256]{2,1,0:T(8,128)(2,1)S(1)}, u32[]{:S(2)}, u32[]{:S(2)}) collective-permute-start(bf16[4,512,256]{2,1,0:T(8,128)(2,1)S(1)} %pad_maximum_fusion), channel_id=1, source_target_pairs={{0,33},{1,32},{32,1},{33,0},{2,35},{3,34},{34,3},{35,2},{4,37},{5,... | collective-permute-start | bytes 3145736 | tf_op jit(solution)/shard_map/ppermute | solution.py:92
  114.6 5.8 %collective-permute-start.4 = (bf16[8,512,256]{2,1,0:T(8,128)(2,1)S(1)}, bf16[8,512,256]{2,1,0:T(8,128)(2,1)}, u32[]{:S(2)}, u32[]{:S(2)}) collective-permute-start(bf16[8,512,256]{2,1,0:T(8,128)(2,1)S(1)} %constant_dynamic-update-slice_fusion.near_ref), channel_id=1, source_target_pairs={{0,16},{16,0},{1,17},{17,1},{2,18},{18,2},{3,19},{19,3},{4,20},{20... | collective-permute-start | bytes 6291464 | tf_op jit(solution)/shard_map/ppermute | solution.py:92

commit v2 on v1

v2 whole, which is shorter than its diff:
```python
import jax
import jax.numpy as jnp
from jax import lax
from jax.experimental import pallas as pl
from jax.experimental.pallas import tpu as pltpu
from jax.sharding import Mesh, PartitionSpec as P

BLK = 512
SHIFT = 0.001
DP = ("x", "yl", "core")
EVERY = ("x", "yl", "core", "prec", "pair")
ROWS_BY_ROWS = (((1,), (1,)), ((), ()))
ROWS_BY_COLUMNS = (((1,), (0,)), ((), ()))
CUT_LIMIT = 48 << 20
HALF_LIMIT = 24 << 20
VMEM_LIMIT = 24 << 20
GRAFT_LIMIT = 8 << 20
HALF = 128
GROUPS = tuple(
    tuple(4 * x + offset for x in some) for offset in (0, 2, 1, 3) for some in ((0, 1, 3), (2,))
)


def dot(left, right, contract=ROWS_BY_COLUMNS):
    return lax.dot_general(left, right, contract, preferred_element_type=jnp.float32)


def split(matrix):
    high = matrix.astype(jnp.bfloat16)
    return high, (matrix - high.astype(jnp.float32)).astype(jnp.bfloat16)


def product(left, right, contract=ROWS_BY_COLUMNS):
    (left_high, left_low), (right_high, right_low) = left, right
    return dot(left_high, right_high, contract) + (
        dot(left_high, right_low, contract) + dot(left_low, right_high, contract)
    )


def cut_step(place_ref, grads_ref, out_ref, sems):
    first = pl.multiple_of(place_ref[0, 2] * HALF, HALF)
    copies = []
    for shard in range(out_ref.shape[0]):
        source = grads_ref.at[pl.ds(first, HALF), pl.ds(shard * BLK, BLK)]
        copies.append(pltpu.make_async_copy(source, out_ref.at[shard], sems.at[shard]))
    for copy in copies:
        copy.start()
    for copy in copies:
        copy.wait()


def cut(place, grads):
    shards = grads.shape[1] // BLK
    return pl.pallas_call(
        cut_step,
        out_shape=jax.ShapeDtypeStruct((shards, HALF, BLK), grads.dtype),
        in_specs=[pl.BlockSpec(memory_space=pltpu.SMEM), pl.BlockSpec(memory_space=pl.ANY)],
        out_specs=pl.BlockSpec(memory_space=pltpu.VMEM),
        scratch_shapes=[pltpu.SemaphoreType.DMA((shards,))],
        compiler_params=pltpu.CompilerParams(vmem_limit_bytes=CUT_LIMIT),
    )(place, grads)


def half_step(place_ref, mine_ref, *refs):
    acts, (partial_ref, rest_ref, acts_ref) = refs[:-3], refs[-3:]
    shard, odd = place_ref[0, 1], place_ref[0, 2]
    mine = pl.ds(pl.multiple_of(odd * HALF, HALF), HALF)
    theirs = pl.ds(pl.multiple_of((1 - odd) * HALF, HALF), HALF)
    for group, group_ref in enumerate(acts):
        for slot, bits in enumerate(GROUPS[group]):
            columns = pl.ds(pl.multiple_of((shard ^ bits) * HALF, HALF), HALF)
            acts_ref[:, columns] = group_ref[slot, :, mine]
            rest_ref[:, columns] = group_ref[slot, :, theirs]
    shards = mine_ref.shape[0]
    partial_ref[...] = dot(acts_ref[...], mine_ref[...].reshape(shards * HALF, BLK))


def half_gradient(place, mine, acts):
    vmem = pl.BlockSpec(memory_space=pltpu.VMEM)
    tokens = mine.shape[0] * HALF
    return pl.pallas_call(
        half_step,
        out_shape=(
            jax.ShapeDtypeStruct((BLK, BLK), jnp.float32),
            jax.ShapeDtypeStruct((BLK, tokens), mine.dtype),
        ),
        in_specs=[pl.BlockSpec(memory_space=pltpu.SMEM)] + [vmem] * (1 + len(acts)),
        out_specs=(vmem, vmem),
        scratch_shapes=[pltpu.VMEM((BLK, tokens), mine.dtype)],
        compiler_params=pltpu.CompilerParams(vmem_limit_bytes=HALF_LIMIT),
    )(place, mine, *acts)


def block_step(place_ref, partial_ref, rest_ref, first_ref, second_ref, update_ref, sums_ref, root_ref):
    some = rest_ref.shape[1] // 2
    transposed = (
        partial_ref[...]
        + dot(rest_ref[:, :some], first_ref[...].reshape(some, BLK))
        + dot(rest_ref[:, some:], second_ref[...].reshape(some, BLK))
    )
    parts = split(transposed)
    statistic = product(parts, parts, ROWS_BY_ROWS)
    grad_parts = split(transposed.T)
    on_diagonal = lax.broadcasted_iota(jnp.int32, (BLK, BLK), 0) == lax.broadcasted_iota(
        jnp.int32, (BLK, BLK), 1
    )
    shifted = statistic + jnp.where(on_diagonal, jnp.float32(SHIFT), jnp.float32(0.0))
    scaling = 2.5 / jnp.sqrt(jnp.sum(shifted * shifted) + 1e-06)
    root_ref[...] = jnp.where(on_diagonal, jnp.float32(1.25), jnp.float32(0.0)) - (
        0.25 * scaling
    ) * shifted

    @pl.when(place_ref[0, 0] == 2)
    def _():
        factor = root_ref[...]
        factor_parts = split(factor)
        square = product(factor_parts, factor_parts)
        square_parts = split(square)
        fourth = product(square_parts, square_parts)
        root_ref[...] = 1.25 * factor + product(split(fourth), split(square - 1.25 * factor))

    root_parts = split(root_ref[...])
    half = product(grad_parts, root_parts)
    update = product(split(half), root_parts) * jnp.sqrt(scaling)
    update_ref[...] = update
    lane = lax.broadcasted_iota(jnp.int32, sums_ref.shape, 2)
    grad_squares = jnp.sum(transposed * transposed)
    update_squares = jnp.sum(update * update)
    sums_ref[...] = jnp.where(lane == 0, grad_squares, jnp.where(lane == 1, update_squares, 0.0))


def run_block(place, partial, rest, first, second, devices):
    vmem = pl.BlockSpec(memory_space=pltpu.VMEM)
    return pl.pallas_call(
        block_step,
        out_shape=(
            jax.ShapeDtypeStruct((BLK, BLK), jnp.float32),
            jax.ShapeDtypeStruct((devices, 1, 128), jnp.float32),
        ),
        in_specs=[pl.BlockSpec(memory_space=pltpu.SMEM)] + [vmem] * 4,
        out_specs=(vmem, vmem),
        scratch_shapes=[pltpu.VMEM((BLK, BLK), jnp.float32)],
        compiler_params=pltpu.CompilerParams(vmem_limit_bytes=VMEM_LIMIT),
    )(place, partial, rest, first, second)


def graft_step(sums_ref, update_ref, out_ref):
    totals = jnp.sum(sums_ref[...], axis=0)
    lane = lax.broadcasted_iota(jnp.int32, totals.shape, 1)
    grad_squares = jnp.sum(jnp.where(lane == 0, totals, 0.0))
    update_squares = jnp.sum(jnp.where(lane == 1, totals, 0.0))
    out_ref[...] = update_ref[...] * jnp.sqrt(grad_squares / update_squares)


def graft(sums, update):
    vmem = pl.BlockSpec(memory_space=pltpu.VMEM)
    return pl.pallas_call(
        graft_step,
        out_shape=jax.ShapeDtypeStruct(update.shape, update.dtype),
        in_specs=[vmem, vmem],
        out_specs=vmem,
        compiler_params=pltpu.CompilerParams(vmem_limit_bytes=GRAFT_LIMIT),
    )(sums, update)


def swap(value, axes, bits):
    size = 1
    for axis in axes:
        size *= lax.axis_size(axis)
    return lax.ppermute(value, axes, [(i, i ^ bits) for i in range(size)])


def swap_planes(value, up):
    step = 1 if up else -1
    pairs = [(i, (i + (step if i % 2 == 0 else -step)) % 8) for i in range(8)]
    return lax.ppermute(value, "prec", pairs)


def per_device(activations, output_grads, iter_counts):
    odd = lax.axis_index("prec") % 2
    place = jnp.stack([iter_counts[0, 0], lax.axis_index(DP), odd]).reshape(1, 3).astype(jnp.int32)
    own = activations.T
    near = [swap(own, ("x",), bits) for bits in (1, 3)]
    mine = cut(place, output_grads)
    three = jnp.stack([own] + near)
    mine, three = lax.optimization_barrier((mine, three))
    mine = lax.all_to_all(mine, DP, 0, 0, tiled=True)
    last = swap(three[1:2], ("x",), 3)
    acts = [three, last] + [swap(value, ("yl", "pair"), 3) for value in (three, last)]
    acts += [swap(value, ("core",), 1) for value in acts]
    half = mine.shape[0] // 2
    first, second = swap_planes(mine[:half], True), swap_planes(mine[half:], False)
    partial, rest = half_gradient(place, mine, acts)

    devices = 256
    update, sums = run_block(place, partial, rest, first, second, devices)
    sums = lax.all_to_all(sums, EVERY, 0, 0, tiled=True)
    return graft(sums, update)


def solution(mesh):
    fine = Mesh(mesh.devices.reshape(4, 2, 2, 8, 2), EVERY)
    in_specs = (P(DP, "prec"), P(DP, "pair"), P(("pair",) + DP, "prec"))
    out_specs = P(("pair",) + DP, "prec")
    return jax.shard_map(
        per_device, mesh=fine, in_specs=in_specs, out_specs=out_specs, check_vma=False
    )
```

time: 159 us -> 107 us (0.67)
  waiting for transfers between devices: 92.8 us -> 36 us
  starting transfers between devices: 13.6 us -> 28 us
  local copies, waits for them, and re-layouts: 13.8 us -> 2.56 us
  Pallas kernels: 8.77 us -> 13 us
    ppermute x5 -> x9, waiting for transfers between devices: 92.8 us -> 9.72 us  [swap(): return lax.ppermute(value, axes, [(i, i ^ bits) for i in range(size)])]
    all_to_all x1, waiting for transfers between devices: 0.01 us -> 21.6 us  [per_device(): mine = lax.all_to_all(mine, DP, 0, 0, tiled=True)]
    ppermute x5 -> x9, starting transfers between devices: 5.94 us -> 15.7 us  [swap(): return lax.ppermute(value, axes, [(i, i ^ bits) for i in range(size)])]
    pallas_call x0 -> x3, Pallas kernels: none -> 7.45 us  [the longest x1 3.64 us: half_gradient(): pl.pallas_call(half_step, out_shape=(jax.ShapeDtypeStruct((BLK, BLK), jnp...]
    reshape x1 -> x0, local copies, waits for them, and re-layouts: 6.39 us -> none  [per_device(): pieces = output_grads.reshape(tokens, shards, BLK).transpose(1, 0, 2)]
    ppermute x0 -> x2, starting transfers between devices: none -> 5.66 us  [swap_planes(): return lax.ppermute(value, 'prec', pairs)]
    ppermute x0 -> x2, waiting for transfers between devices: none -> 4.69 us  [swap_planes(): return lax.ppermute(value, 'prec', pairs)]
    unnamed x8 -> x3, local copies, waits for them, and re-layouts: 6.63 us -> 2.4 us
  transfers between devices with their start and end apart: 6 -> 12, of which waited for: 4 -> 7; matrix products, arithmetic and copies ran while one was open for 0% -> 0% of each run, Pallas kernels for 0% -> 6%
where the time goes in v2:
time: 107 us; the launch traced here: 106 us
  waiting for transfers between devices  36 us (34%)
  starting transfers between devices  28 us (26%)
  blocking collectives  25.9 us (24%)
  Pallas kernels  13 us (12%)
  local copies, waits for them, and re-layouts  2.56 us (2%)
    all_to_all x1, blocking collectives, per_device(): sums = lax.all_to_all(sums, EVERY, 0, 0, tiled=True)  25.9 us
    all_to_all x1, waiting for transfers between devices, per_device(): mine = lax.all_to_all(mine, DP, 0, 0, tiled=True)  21.6 us
    ppermute x9, starting transfers between devices, swap(): return lax.ppermute(value, axes, [(i, i ^ bits) for i in range(size)])  15.7 us
    ppermute x9, waiting for transfers between devices, swap(): return lax.ppermute(value, axes, [(i, i ^ bits) for i in range(size)])  9.72 us
    all_to_all x1, starting transfers between devices, per_device(): mine = lax.all_to_all(mine, DP, 0, 0, tiled=True)  6.63 us
    ppermute x2, starting transfers between devices, swap_planes(): return lax.ppermute(value, 'prec', pairs)  5.66 us
    pallas_call x1, Pallas kernels, run_block(): pl.pallas_call(block_step, out_shape=(jax.ShapeDtypeStruct((BLK, BLK), jn...  5.56 us
    ppermute x2, waiting for transfers between devices, swap_planes(): return lax.ppermute(value, 'prec', pairs)  4.69 us
  transfers between devices with their start and end apart: 12, of which 7 were waited for; matrix products, arithmetic and copies ran while one was open for 0% of the time, Pallas kernels for 6%

profile of v2, /device:TPU:1, one launch (start us, length us, event | category | flops | bytes accessed | tf_op | source)
XLA Modules:
  0.0 106.4 jit_solution(8075713340201537277)
XLA Ops:
  0.0 1.1 %copy.4 = bf16[256,512]{0,1:T(8,128)(2,1)S(1)} copy(bf16[256,512]{1,0:T(8,128)(2,1)} %param.3) | data formatting | bytes 524288 | tf_op args[0]
  1.1 2.1 %collective-permute-start = (bf16[512,256]{1,0:T(8,128)(2,1)S(1)}, bf16[512,256]{1,0:T(8,128)(2,1)S(1)}, u32[]{:S(2)}, u32[]{:S(2)}) collective-permute-start(bf16[512,256]{1,0:T(8,128)(2,1)S(1)} %bitcast.11), channel_id=1, source_target_pairs={{0,64},{64,0},{128,192},{192,128},{1,65},{65,1},{129,193},{193,129... | collective-permute-start | bytes 786440 | tf_op jit(solution)/shard_map/ppermute | solution.py:170
  3.2 1.8 %collective-permute-start.1 = (bf16[512,256]{1,0:T(8,128)(2,1)S(1)}, bf16[512,256]{1,0:T(8,128)(2,1)S(1)}, u32[]{:S(2)}, u32[]{:S(2)}) collective-permute-start(bf16[512,256]{1,0:T(8,128)(2,1)S(1)} %bitcast.12), channel_id=1, source_target_pairs={{0,192},{64,128},{128,64},{192,0},{1,193},{65,129},{129,65},{193,1... | collective-permute-start | bytes 786440 | tf_op jit(solution)/shard_map/ppermute | solution.py:170
  5.7 0.1 add_bitcast_fusion.place_ref
  5.8 2.3 %shard_map.37 = bf16[16,128,512]{2,1,0:T(8,128)(2,1)S(1)} custom-call(s32[1,3]{1,0:T(1,128)S(1)} %add_bitcast_fusion.place_ref, bf16[256,8192]{1,0:T(8,128)(2,1)} %grads_ref.1), custom_call_target="tpu_custom_call" | custom-call | tf_op jit(solution)/shard_map/pallas_call | solution.py:54
  8.1 0.0 copy-start
  8.1 1.3 %copy-done = bf16[16,128,512]{2,1,0:T(8,128)(2,1)} copy-done((bf16[16,128,512]{2,1,0:T(8,128)(2,1)}, bf16[16,128,512]{2,1,0:T(8,128)(2,1)S(1)}, u32[]{:S(2)}) %copy-start) | copy-done | bytes 2097176
  9.4 0.0 collective-permute-done
  9.4 1.5 %collective-permute-done.1 = bf16[512,256]{1,0:T(8,128)(2,1)S(1)} collective-permute-done((bf16[512,256]{1,0:T(8,128)(2,1)S(1)}, bf16[512,256]{1,0:T(8,128)(2,1)S(1)}, u32[]{:S(2)}, u32[]{:S(2)}) %collective-permute-start.1) | collective-permute-done | bytes 262176 | tf_op jit(solution)/shard_map/ppermute | solution.py:170
  10.9 0.1 pad_maximum_fusion.refs_0_
  11.0 6.6 %all-to-all-start = ((bf16[16,128,512]{2,1,0:T(8,128)(2,1)}), bf16[16,128,512]{2,1,0:T(8,128)(2,1)S(1)}, u32[]{:S(2)}, u32[]{:S(2)}) async-start(bf16[16,128,512]{2,1,0:T(8,128)(2,1)} %copy-done), calls=%async_computation | async-start | bytes 4194304 | tf_op jit(solution)/shard_map/all_to_all | solution.py:187
  17.6 2.8 %collective-permute-start.3 = (bf16[3,512,256]{2,1,0:T(8,128)(2,1)S(1)}, bf16[3,512,256]{2,1,0:T(8,128)(2,1)}, u32[]{:S(2)}, u32[]{:S(2)}) collective-permute-start(bf16[3,512,256]{2,1,0:T(8,128)(2,1)S(1)} %pad_maximum_fusion.refs_0_), channel_id=1, source_target_pairs={{0,33},{1,32},{32,1},{33,0},{2,35},{3,34},{34,3},{35,2},{4,37},{5,... | collective-permute-start | bytes 2359304 | tf_op jit(solution)/shard_map/ppermute | solution.py:170
  20.5 2.5 %collective-permute-start.2 = (bf16[1,512,256]{2,1,0:T(8,128)(2,1)S(1)}, bf16[1,512,256]{2,1,0:T(8,128)(2,1)S(1)}, u32[]{:S(2)}, u32[]{:S(2)}) collective-permute-start(bf16[1,512,256]{2,1,0:T(8,128)(2,1)S(1)} %slice.9), channel_id=1, source_target_pairs={{0,192},{64,128},{128,64},{192,0},{1,193},{65,129},{129,65},{193,1... | collective-permute-start | bytes 786440 | tf_op jit(solution)/shard_map/ppermute | solution.py:170
  23.0 21.6 %all-to-all-done.mine_ref = bf16[16,128,512]{2,1,0:T(8,128)(2,1)S(1)} async-done(((bf16[16,128,512]{2,1,0:T(8,128)(2,1)}), bf16[16,128,512]{2,1,0:T(8,128)(2,1)S(1)}, u32[]{:S(2)}, u32[]{:S(2)}) %all-to-all-start) | async-done | bytes 2097184 | tf_op jit(solution)/shard_map/all_to_all | solution.py:187
  44.6 0.1 fusion
  44.7 5.7 %collective-permute-start.10 = (bf16[8,128,512]{2,1,0:T(8,128)(2,1)S(1)}, bf16[8,128,512]{2,1,0:T(8,128)(2,1)S(1)}, u32[]{:S(2)}, u32[]{:S(2)}) collective-permute-start(bf16[8,128,512]{2,1,0:T(8,128)(2,1)S(1)} %get-tuple-element.17), channel_id=1, source_target_pairs={{0,14},{2,4},{4,2},{6,8},{8,6},{10,12},{12,10},{14,0},{1,15},{3,5}... | collective-permute-start | bytes 3145736 | tf_op jit(solution)/shard_map/ppermute | solution.py:176
  50.4 0.0 collective-permute-start.9
  50.4 0.0 collective-permute-done.2.refs_1_
  50.4 1.6 %collective-permute-start.6 = (bf16[1,512,256]{2,1,0:T(8,128)(2,1)S(1)}, bf16[1,512,256]{2,1,0:T(8,128)(2,1)S(1)}, u32[]{:S(2)}, u32[]{:S(2)}) collective-permute-start(bf16[1,512,256]{2,1,0:T(8,128)(2,1)S(1)} %collective-permute-done.2.refs_1_), channel_id=1, source_target_pairs={{0,16},{16,0},{1,17},{17,1},{2,18},{18,2},{3,19},{19,3},{4,20},{20... | collective-permute-start | bytes 786440 | tf_op jit(solution)/shard_map/ppermute | solution.py:170
  52.0 0.1 collective-permute-start.5
  52.1 0.0 collective-permute-done.3.refs_2_
  52.1 0.4 collective-permute-start.7
  52.5 0.6 collective-permute-done.6.refs_5_
  53.2 3.5 %collective-permute-start.4 = (bf16[1,512,256]{2,1,0:T(8,128)(2,1)S(1)}, bf16[1,512,256]{2,1,0:T(8,128)(2,1)S(1)}, u32[]{:S(2)}, u32[]{:S(2)}) collective-permute-start(bf16[1,512,256]{2,1,0:T(8,128)(2,1)S(1)} %collective-permute-done.2.refs_1_), channel_id=1, source_target_pairs={{0,33},{1,32},{32,1},{33,0},{2,35},{3,34},{34,3},{35,2},{4,37},{5,... | collective-permute-start | bytes 786440 | tf_op jit(solution)/shard_map/ppermute | solution.py:170
  56.7 6.4 %collective-permute-done.4.refs_3_ = bf16[1,512,256]{2,1,0:T(8,128)(2,1)S(1)} collective-permute-done((bf16[1,512,256]{2,1,0:T(8,128)(2,1)S(1)}, bf16[1,512,256]{2,1,0:T(8,128)(2,1)S(1)}, u32[]{:S(2)}, u32[]{:S(2)}) %collective-permute-start.4) | collective-permute-done | bytes 262176 | tf_op jit(solution)/shard_map/ppermute | solution.py:170
  63.0 0.9 collective-permute-start.8
  63.9 1.2 %collective-permute-done.8.refs_7_ = bf16[1,512,256]{2,1,0:T(8,128)(2,1)S(1)} collective-permute-done((bf16[1,512,256]{2,1,0:T(8,128)(2,1)S(1)}, bf16[1,512,256]{2,1,0:T(8,128)(2,1)S(1)}, u32[]{:S(2)}, u32[]{:S(2)}) %collective-permute-start.8) | collective-permute-done | bytes 262176 | tf_op jit(solution)/shard_map/ppermute | solution.py:170
  65.1 0.0 collective-permute-done.5.refs_4_
  65.1 0.0 collective-permute-done.7.refs_6_
  65.1 3.6 %shard_map.38 = (f32[512,512]{1,0:T(8,128)S(1)}, bf16[512,2048]{1,0:T(8,128)(2,1)S(1)}) custom-call(s32[1,3]{1,0:T(1,128)S(1)} %add_bitcast_fusion.place_ref, bf16[16,128,512]{2,1,0:T(8,128)(2,1)S(1)} %all-to-all-done.mine_ref, bf16[3,512,256]{2,1,0:T(8,128)(2,1)S(1)} %pad_maximum_fusion.refs_0_, bf16[1,512,256]{2,1,0:T(8,128)(2,1)S(1)} %collective-permute-done.2.refs_1_, ...), custom_call_target="tpu_custom_call" | custom-call | tf_op jit(solution)/shard_map/pallas_call | solution.py:81
  68.7 3.8 %collective-permute-done.10.second_ref = bf16[8,128,512]{2,1,0:T(8,128)(2,1)S(1)} collective-permute-done((bf16[8,128,512]{2,1,0:T(8,128)(2,1)S(1)}, bf16[8,128,512]{2,1,0:T(8,128)(2,1)S(1)}, u32[]{:S(2)}, u32[]{:S(2)}) %collective-permute-start.10) | collective-permute-done | bytes 1048608 | tf_op jit(solution)/shard_map/ppermute | solution.py:176
  72.5 0.9 collective-permute-done.9.first_ref
  73.4 5.6 %shard_map.39 = (f32[512,512]{1,0:T(8,128)S(1)}, f32[256,1,128]{2,1,0:T(1,128)S(1)}) custom-call(s32[1,3]{1,0:T(1,128)S(1)} %add_bitcast_fusion.place_ref, f32[512,512]{1,0:T(8,128)S(1)} %get-tuple-element.13.partial_ref, bf16[512,2048]{1,0:T(8,128)(2,1)S(1)} %get-tuple-element.14.rest_ref, bf16[8,128,512]{2,1,0:T(8,128)(2,1)S(1)} %collective-permute-done.9.first_ref, ...), custom_call_target="tpu_custom_call" | custom-call | tf_op jit(solution)/shard_map/pallas_call | solution.py:134
  79.0 25.9 %all_to_all.10.sums_ref = f32[256,1,128]{2,1,0:T(1,128)S(1)} all-to-all(f32[256,1,128]{2,1,0:T(1,128)S(1)} %get-tuple-element.15), channel_id=1, replica_groups=mesh['x'=4,'yl'=2,'core'=2,'prec'=8,'pair'=2] {'x','yl','core','prec','p..., dimensions={0} | all-to-all | bytes 262144 | tf_op jit(solution)/shard_map/all_to_all | solution.py:197
  104.8 1.5 %shard_map.40 = f32[512,512]{1,0:T(8,128)} custom-call(f32[256,1,128]{2,1,0:T(1,128)S(1)} %all_to_all.10.sums_ref, f32[512,512]{1,0:T(8,128)S(1)} %get-tuple-element.16.update_ref), custom_call_target="tpu_custom_call" | custom-call | tf_op jit(solution)/shard_map/pallas_call | solution.py:157
  (1 shorter events, 0.0 us)
Async XLA Ops:
  1.1 8.3 %collective-permute-start = (bf16[512,256]{1,0:T(8,128)(2,1)S(1)}, bf16[512,256]{1,0:T(8,128)(2,1)S(1)}, u32[]{:S(2)}, u32[]{:S(2)}) collective-permute-start(bf16[512,256]{1,0:T(8,128)(2,1)S(1)} %bitcast.11), channel_id=1, source_target_pairs={{0,64},{64,0},{128,192},{192,128},{1,65},{65,1},{129,193},{193,129... | collective-permute-start | bytes 786440 | tf_op jit(solution)/shard_map/ppermute | solution.py:170
  3.2 7.7 %collective-permute-start.1 = (bf16[512,256]{1,0:T(8,128)(2,1)S(1)}, bf16[512,256]{1,0:T(8,128)(2,1)S(1)}, u32[]{:S(2)}, u32[]{:S(2)}) collective-permute-start(bf16[512,256]{1,0:T(8,128)(2,1)S(1)} %bitcast.12), channel_id=1, source_target_pairs={{0,192},{64,128},{128,64},{192,0},{1,193},{65,129},{129,65},{193,1... | collective-permute-start | bytes 786440 | tf_op jit(solution)/shard_map/ppermute | solution.py:170
  8.1 1.3 %copy-start = (bf16[16,128,512]{2,1,0:T(8,128)(2,1)}, bf16[16,128,512]{2,1,0:T(8,128)(2,1)S(1)}, u32[]{:S(2)}) copy-start(bf16[16,128,512]{2,1,0:T(8,128)(2,1)S(1)} %shard_map.37) | copy-start | bytes 6291460
  11.0 33.6 %all-to-all-start = ((bf16[16,128,512]{2,1,0:T(8,128)(2,1)}), bf16[16,128,512]{2,1,0:T(8,128)(2,1)S(1)}, u32[]{:S(2)}, u32[]{:S(2)}) async-start(bf16[16,128,512]{2,1,0:T(8,128)(2,1)} %copy-done), calls=%async_computation | async-start | bytes 4194304 | tf_op jit(solution)/shard_map/all_to_all | solution.py:187
  17.6 34.5 %collective-permute-start.3 = (bf16[3,512,256]{2,1,0:T(8,128)(2,1)S(1)}, bf16[3,512,256]{2,1,0:T(8,128)(2,1)}, u32[]{:S(2)}, u32[]{:S(2)}) collective-permute-start(bf16[3,512,256]{2,1,0:T(8,128)(2,1)S(1)} %pad_maximum_fusion.refs_0_), channel_id=1, source_target_pairs={{0,33},{1,32},{32,1},{33,0},{2,35},{3,34},{34,3},{35,2},{4,37},{5,... | collective-permute-start | bytes 2359304 | tf_op jit(solution)/shard_map/ppermute | solution.py:170
  20.5 29.9 %collective-permute-start.2 = (bf16[1,512,256]{2,1,0:T(8,128)(2,1)S(1)}, bf16[1,512,256]{2,1,0:T(8,128)(2,1)S(1)}, u32[]{:S(2)}, u32[]{:S(2)}) collective-permute-start(bf16[1,512,256]{2,1,0:T(8,128)(2,1)S(1)} %slice.9), channel_id=1, source_target_pairs={{0,192},{64,128},{128,64},{192,0},{1,193},{65,129},{129,65},{193,1... | collective-permute-start | bytes 786440 | tf_op jit(solution)/shard_map/ppermute | solution.py:170
  44.7 27.8 %collective-permute-start.10 = (bf16[8,128,512]{2,1,0:T(8,128)(2,1)S(1)}, bf16[8,128,512]{2,1,0:T(8,128)(2,1)S(1)}, u32[]{:S(2)}, u32[]{:S(2)}) collective-permute-start(bf16[8,128,512]{2,1,0:T(8,128)(2,1)S(1)} %get-tuple-element.17), channel_id=1, source_target_pairs={{0,14},{2,4},{4,2},{6,8},{8,6},{10,12},{12,10},{14,0},{1,15},{3,5}... | collective-permute-start | bytes 3145736 | tf_op jit(solution)/shard_map/ppermute | solution.py:176
  50.4 23.0 %collective-permute-start.9 = (bf16[8,128,512]{2,1,0:T(8,128)(2,1)S(1)}, bf16[8,128,512]{2,1,0:T(8,128)(2,1)S(1)}, u32[]{:S(2)}, u32[]{:S(2)}) collective-permute-start(bf16[8,128,512]{2,1,0:T(8,128)(2,1)S(1)} %get-tuple-element.18), channel_id=1, source_target_pairs={{0,2},{2,0},{4,6},{6,4},{8,10},{10,8},{12,14},{14,12},{1,3},{3,1},... | collective-permute-start | bytes 3145736 | tf_op jit(solution)/shard_map/ppermute | solution.py:176
  50.4 2.8 %collective-permute-start.6 = (bf16[1,512,256]{2,1,0:T(8,128)(2,1)S(1)}, bf16[1,512,256]{2,1,0:T(8,128)(2,1)S(1)}, u32[]{:S(2)}, u32[]{:S(2)}) collective-permute-start(bf16[1,512,256]{2,1,0:T(8,128)(2,1)S(1)} %collective-permute-done.2.refs_1_), channel_id=1, source_target_pairs={{0,16},{16,0},{1,17},{17,1},{2,18},{18,2},{3,19},{19,3},{4,20},{20... | collective-permute-start | bytes 786440 | tf_op jit(solution)/shard_map/ppermute | solution.py:170
  52.0 13.1 %collective-permute-start.5 = (bf16[3,512,256]{2,1,0:T(8,128)(2,1)S(1)}, bf16[3,512,256]{2,1,0:T(8,128)(2,1)S(1)}, u32[]{:S(2)}, u32[]{:S(2)}) collective-permute-start(bf16[3,512,256]{2,1,0:T(8,128)(2,1)S(1)} %pad_maximum_fusion.refs_0_), channel_id=1, source_target_pairs={{0,16},{16,0},{1,17},{17,1},{2,18},{18,2},{3,19},{19,3},{4,20},{20... | collective-permute-start | bytes 2359304 | tf_op jit(solution)/shard_map/ppermute | solution.py:170
  52.1 13.0 %collective-permute-start.7 = (bf16[3,512,256]{2,1,0:T(8,128)(2,1)}, bf16[3,512,256]{2,1,0:T(8,128)(2,1)S(1)}, u32[]{:S(2)}, u32[]{:S(2)}) collective-permute-start(bf16[3,512,256]{2,1,0:T(8,128)(2,1)} %collective-permute-done.3.refs_2_), channel_id=1, source_target_pairs={{0,16},{16,0},{1,17},{17,1},{2,18},{18,2},{3,19},{19,3},{4,20},{20... | collective-permute-start | bytes 2359304 | tf_op jit(solution)/shard_map/ppermute | solution.py:170
  53.2 9.9 %collective-permute-start.4 = (bf16[1,512,256]{2,1,0:T(8,128)(2,1)S(1)}, bf16[1,512,256]{2,1,0:T(8,128)(2,1)S(1)}, u32[]{:S(2)}, u32[]{:S(2)}) collective-permute-start(bf16[1,512,256]{2,1,0:T(8,128)(2,1)S(1)} %collective-permute-done.2.refs_1_), channel_id=1, source_target_pairs={{0,33},{1,32},{32,1},{33,0},{2,35},{3,34},{34,3},{35,2},{4,37},{5,... | collective-permute-start | bytes 786440 | tf_op jit(solution)/shard_map/ppermute | solution.py:170
  63.0 2.0 %collective-permute-start.8 = (bf16[1,512,256]{2,1,0:T(8,128)(2,1)S(1)}, bf16[1,512,256]{2,1,0:T(8,128)(2,1)S(1)}, u32[]{:S(2)}, u32[]{:S(2)}) collective-permute-start(bf16[1,512,256]{2,1,0:T(8,128)(2,1)S(1)} %collective-permute-done.4.refs_3_), channel_id=1, source_target_pairs={{0,16},{16,0},{1,17},{17,1},{2,18},{18,2},{3,19},{19,3},{4,20},{20... | collective-permute-start | bytes 786440 | tf_op jit(solution)/shard_map/ppermute | solution.py:170

commit v3 on v2

--- a/solution.py
+++ b/solution.py
@@ -15,7 +15,11 @@
 HALF_LIMIT = 24 << 20
 VMEM_LIMIT = 24 << 20
 GRAFT_LIMIT = 8 << 20
+PICK_LIMIT = 8 << 20
 HALF = 128
+NEAR = (0, 4, 12, 2)
+FAR = ((8, 9, 6, 7), (10, 11, 14, 15))
+ORDER = NEAR + tuple(bits + 1 for bits in NEAR) + FAR[0] + FAR[1]
 GROUPS = tuple(
     tuple(4 * x + offset for x in some) for offset in (0, 2, 1, 3) for some in ((0, 1, 3), (2,))
 )
@@ -37,12 +41,22 @@
     )
 
 
-def cut_step(place_ref, grads_ref, out_ref, sems):
-    first = pl.multiple_of(place_ref[0, 2] * HALF, HALF)
+def cut_step(place_ref, grads_ref, mine_ref, *refs):
+    near, sems = refs[:-1], refs[-1]
+    shard, odd = place_ref[0, 1], place_ref[0, 2]
+    mine = pl.ds(pl.multiple_of(odd * HALF, HALF), HALF)
+    theirs = pl.ds(pl.multiple_of((1 - odd) * HALF, HALF), HALF)
+    shards = mine_ref.shape[0]
     copies = []
-    for shard in range(out_ref.shape[0]):
-        source = grads_ref.at[pl.ds(first, HALF), pl.ds(shard * BLK, BLK)]
-        copies.append(pltpu.make_async_copy(source, out_ref.at[shard], sems.at[shard]))
+    for step in range(shards):
+        source = grads_ref.at[mine, pl.ds(step * BLK, BLK)]
+        copies.append(pltpu.make_async_copy(source, mine_ref.at[step], sems.at[step]))
+    for slot, out_ref in enumerate(near):
+        for core in range(2):
+            block = shard ^ (NEAR[slot] + core)
+            source = grads_ref.at[theirs, pl.ds(pl.multiple_of(block * BLK, BLK), BLK)]
+            sem = sems.at[shards + 2 * slot + core]
+            copies.append(pltpu.make_async_copy(source, out_ref.at[core], sem))
     for copy in copies:
         copy.start()
     for copy in copies:
@@ -51,14 +65,33 @@
 
 def cut(place, grads):
     shards = grads.shape[1] // BLK
+    near = jax.ShapeDtypeStruct((2, HALF, BLK), grads.dtype)
     return pl.pallas_call(
         cut_step,
-        out_shape=jax.ShapeDtypeStruct((shards, HALF, BLK), grads.dtype),
+        out_shape=[jax.ShapeDtypeStruct((shards, HALF, BLK), grads.dtype)] + [near] * len(NEAR),
         in_specs=[pl.BlockSpec(memory_space=pltpu.SMEM), pl.BlockSpec(memory_space=pl.ANY)],
-        out_specs=pl.BlockSpec(memory_space=pltpu.VMEM),
-        scratch_shapes=[pltpu.SemaphoreType.DMA((shards,))],
+        out_specs=[pl.BlockSpec(memory_space=pltpu.VMEM)] * (1 + len(NEAR)),
+        scratch_shapes=[pltpu.SemaphoreType.DMA((shards + 2 * len(NEAR),))],
         compiler_params=pltpu.CompilerParams(vmem_limit_bytes=CUT_LIMIT),
     )(place, grads)
+
+
+def pick_step(place_ref, mine_ref, *outs):
+    shard = place_ref[0, 1]
+    for out_ref, some in zip(outs, FAR, strict=True):
+        for slot, bits in enumerate(some):
+            out_ref[slot] = mine_ref[shard ^ bits]
+
+
+def pick(place, mine):
+    vmem = pl.BlockSpec(memory_space=pltpu.VMEM)
+    return pl.pallas_call(
+        pick_step,
+        out_shape=[jax.ShapeDtypeStruct((len(some),) + mine.shape[1:], mine.dtype) for some in FAR],
+        in_specs=[pl.BlockSpec(memory_space=pltpu.SMEM), vmem],
+        out_specs=[vmem] * len(FAR),
+        compiler_params=pltpu.CompilerParams(vmem_limit_bytes=PICK_LIMIT),
+    )(place, mine)
 
 
 def half_step(place_ref, mine_ref, *refs):
@@ -70,7 +103,7 @@
         for slot, bits in enumerate(GROUPS[group]):
             columns = pl.ds(pl.multiple_of((shard ^ bits) * HALF, HALF), HALF)
             acts_ref[:, columns] = group_ref[slot, :, mine]
-            rest_ref[:, columns] = group_ref[slot, :, theirs]
+            rest_ref[:, pl.ds(ORDER.index(bits) * HALF, HALF)] = group_ref[slot, :, theirs]
     shards = mine_ref.shape[0]
     partial_ref[...] = dot(acts_ref[...], mine_ref[...].reshape(shards * HALF, BLK))
 
@@ -91,13 +124,15 @@
     )(place, mine, *acts)
 
 
-def block_step(place_ref, partial_ref, rest_ref, first_ref, second_ref, update_ref, sums_ref, root_ref):
-    some = rest_ref.shape[1] // 2
-    transposed = (
-        partial_ref[...]
-        + dot(rest_ref[:, :some], first_ref[...].reshape(some, BLK))
-        + dot(rest_ref[:, some:], second_ref[...].reshape(some, BLK))
-    )
+def block_step(place_ref, partial_ref, rest_ref, *refs):
+    near, others, (update_ref, sums_ref, root_ref) = refs[: len(NEAR)], refs[len(NEAR) : -3], refs[-3:]
+    pieces = [jnp.concatenate([near_ref[0] for near_ref in near], axis=0)]
+    pieces += [other_ref[...].reshape(-1, BLK) for other_ref in others]
+    transposed = partial_ref[...]
+    start = 0
+    for piece in pieces:
+        transposed = transposed + dot(rest_ref[:, start : start + piece.shape[0]], piece)
+        start += piece.shape[0]
     parts = split(transposed)
     statistic = product(parts, parts, ROWS_BY_ROWS)
     grad_parts = split(transposed.T)
@@ -129,7 +164,7 @@
     sums_ref[...] = jnp.where(lane == 0, grad_squares, jnp.where(lane == 1, update_squares, 0.0))
 
 
-def run_block(place, partial, rest, first, second, devices):
+def run_block(place, partial, rest, pieces, devices):
     vmem = pl.BlockSpec(memory_space=pltpu.VMEM)
     return pl.pallas_call(
         block_step,
@@ -137,11 +172,11 @@
             jax.ShapeDtypeStruct((BLK, BLK), jnp.float32),
             jax.ShapeDtypeStruct((devices, 1, 128), jnp.float32),
         ),
-        in_specs=[pl.BlockSpec(memory_space=pltpu.SMEM)] + [vmem] * 4,
+        in_specs=[pl.BlockSpec(memory_space=pltpu.SMEM)] + [vmem] * (2 + len(pieces)),
         out_specs=(vmem, vmem),
         scratch_shapes=[pltpu.VMEM((BLK, BLK), jnp.float32)],
         compiler_params=pltpu.CompilerParams(vmem_limit_bytes=VMEM_LIMIT),
-    )(place, partial, rest, first, second)
+    )(place, partial, rest, *pieces)
 
 
 def graft_step(sums_ref, update_ref, out_ref):
@@ -181,19 +216,30 @@
     place = jnp.stack([iter_counts[0, 0], lax.axis_index(DP), odd]).reshape(1, 3).astype(jnp.int32)
     own = activations.T
     near = [swap(own, ("x",), bits) for bits in (1, 3)]
-    mine = cut(place, output_grads)
+    mine, here, *near_grads = cut(place, output_grads)
     three = jnp.stack([own] + near)
     mine, three = lax.optimization_barrier((mine, three))
     mine = lax.all_to_all(mine, DP, 0, 0, tiled=True)
+    three_y = swap(three, ("yl", "pair"), 3)
     last = swap(three[1:2], ("x",), 3)
-    acts = [three, last] + [swap(value, ("yl", "pair"), 3) for value in (three, last)]
-    acts += [swap(value, ("core",), 1) for value in acts]
-    half = mine.shape[0] // 2
-    first, second = swap_planes(mine[:half], True), swap_planes(mine[half:], False)
+    far_three = [swap(value, ("core",), 1) for value in (three, three_y)]
+    ready, _ = lax.optimization_barrier((mine, far_three))
+    first, second = pick(place, ready)
+    last, _ = lax.optimization_barrier((last, (first, second)))
+    ways = (("x", 1), ("x", 3), ("yl", 1))
+    near_grads, _ = lax.optimization_barrier((near_grads, (first, second)))
+    near_grads = [swap(value, (axis,), bits) for value, (axis, bits) in zip(near_grads, ways, strict=True)]
+    first, second = swap_planes(first, True), swap_planes(second, False)
+    last_y = swap(last, ("yl", "pair"), 3)
+    far_last = [swap(value, ("core",), 1) for value in (last, last_y)]
+    acts = [three, last, three_y, last_y, far_three[0], far_last[0], far_three[1], far_last[1]]
+    near_grads, _ = lax.optimization_barrier((near_grads, (first, second)))
+    near_grads = [here] + near_grads
+    taken = swap(jnp.stack([value[1] for value in near_grads]), ("core",), 1)
     partial, rest = half_gradient(place, mine, acts)
 
     devices = 256
-    update, sums = run_block(place, partial, rest, first, second, devices)
+    update, sums = run_block(place, partial, rest, (*near_grads, taken, first, second), devices)
     sums = lax.all_to_all(sums, EVERY, 0, 0, tiled=True)
     return graft(sums, update)
 

time: 107 us -> 104 us (0.972)
  waiting for transfers between devices: 36 us -> 23.6 us
  starting transfers between devices: 28 us -> 36.2 us
  local copies, waits for them, and re-layouts: 2.56 us -> 7.28 us
  blocking collectives: 25.9 us -> 22.6 us
    all_to_all x1, waiting for transfers between devices: 21.6 us -> 0.01 us  [per_device(): mine = lax.all_to_all(mine, DP, 0, 0, tiled=True)]
    ppermute x9 -> x13, waiting for transfers between devices: 9.72 us -> 23.6 us  [swap(): return lax.ppermute(value, axes, [(i, i ^ bits) for i in range(size)])]
    ppermute x9 -> x13, starting transfers between devices: 15.7 us -> 24.1 us  [swap(): return lax.ppermute(value, axes, [(i, i ^ bits) for i in range(size)])]
    ppermute x2, waiting for transfers between devices: 4.69 us -> 0.01 us  [swap_planes(): return lax.ppermute(value, 'prec', pairs)]
    unnamed x3 -> x21, local copies, waits for them, and re-layouts: 2.4 us -> 6.5 us
    all_to_all x1, blocking collectives: 25.9 us -> 22.6 us  [per_device(): sums = lax.all_to_all(sums, EVERY, 0, 0, tiled=True)]
    pallas_call x1 -> x2, Pallas kernels: 2.3 us -> 3.31 us  [the longest x1 2.69 us: cut(): pl.pallas_call(cut_step, out_shape=[jax.ShapeDtypeStruct((shards, HALF, B...]
  transfers between devices with their start and end apart: 12 -> 16, of which waited for: 7 -> 5; matrix products, arithmetic and copies ran while one was open for 0% -> 1% of each run, Pallas kernels for 6% -> 6%
where the time goes in v3:
time: 104 us
  starting transfers between devices  36.2 us (35%)
  waiting for transfers between devices  23.6 us (23%)
  blocking collectives  22.6 us (22%)
  Pallas kernels  13.2 us (13%)
  local copies, waits for them, and re-layouts  7.28 us (7%)
    ppermute x13, starting transfers between devices, swap(): return lax.ppermute(value, axes, [(i, i ^ bits) for i in range(size)])  24.1 us
    ppermute x13, waiting for transfers between devices, swap(): return lax.ppermute(value, axes, [(i, i ^ bits) for i in range(size)])  23.6 us
    all_to_all x1, blocking collectives, per_device(): sums = lax.all_to_all(sums, EVERY, 0, 0, tiled=True)  22.6 us
    unnamed x21, local copies, waits for them, and re-layouts  6.5 us
    ppermute x2, starting transfers between devices, swap_planes(): return lax.ppermute(value, 'prec', pairs)  6.23 us
    all_to_all x1, starting transfers between devices, per_device(): mine = lax.all_to_all(mine, DP, 0, 0, tiled=True)  5.87 us
    pallas_call x1, Pallas kernels, run_block(): pl.pallas_call(block_step, out_shape=(jax.ShapeDtypeStruct((BLK, BLK), jn...  5.37 us
    pallas_call x1, Pallas kernels, half_gradient(): pl.pallas_call(half_step, out_shape=(jax.ShapeDtypeStruct((BLK, BLK), jnp...  3 us
  transfers between devices with their start and end apart: 16, of which 5 were waited for; matrix products, arithmetic and copies ran while one was open for 1% of the time, Pallas kernels for 6%

profile of v3, /device:TPU:1, one launch (start us, length us, event | category | flops | bytes accessed | tf_op | source)
XLA Modules:
  0.0 103.9 jit_solution(1109291987348140574)
XLA Ops:
  0.0 1.1 %copy.4 = bf16[256,512]{0,1:T(8,128)(2,1)S(1)} copy(bf16[256,512]{1,0:T(8,128)(2,1)} %param.3) | data formatting | bytes 524288 | tf_op args[0]
  1.1 3.4 %collective-permute-start.1 = (bf16[512,256]{1,0:T(8,128)(2,1)S(1)}, bf16[512,256]{1,0:T(8,128)(2,1)S(1)}, u32[]{:S(2)}, u32[]{:S(2)}) collective-permute-start(bf16[512,256]{1,0:T(8,128)(2,1)S(1)} %bitcast.11), channel_id=1, source_target_pairs={{0,192},{64,128},{128,64},{192,0},{1,193},{65,129},{129,65},{193,1... | collective-permute-start | bytes 786440 | tf_op jit(solution)/shard_map/ppermute | solution.py:205
  4.5 0.0 collective-permute-start
  5.1 0.1 add_bitcast_fusion.place_ref
  5.2 2.7 %shard_map.37 = (bf16[16,128,512]{2,1,0:T(8,128)(2,1)S(1)}, bf16[2,128,512]{2,1,0:T(8,128)(2,1)S(1)}, bf16[2,128,512]{2,1,0:T(8,128)(2,1)S(1)}, bf16[2,128,512]{2,1,0:T(8,128)(2,1)S(1)}, bf16[2,128,512]{2,1,0:T(8,128)(2,1)S(1)}) custom-call(s32[1,3]{1,0:T(1,128)S(1)} %add_bitcast_fusion.place_ref, bf16[256,8192]{1,0:T(8,128)(2,1)} %grads_ref.1), custom_call_target="tpu_custom_call" | custom-call | tf_op jit(solution)/shard_map/pallas_call | solution.py:69
  7.9 1.3 %copy-done = bf16[16,128,512]{2,1,0:T(8,128)(2,1)} copy-done((bf16[16,128,512]{2,1,0:T(8,128)(2,1)}, bf16[16,128,512]{2,1,0:T(8,128)(2,1)S(1)}, u32[]{:S(2)}) %copy-start) | copy-done | bytes 2097176
  9.3 0.7 copy-done.7
  10.0 0.7 copy-done.9
  10.7 0.0 collective-permute-done.1
  10.7 0.7 collective-permute-done
  11.3 0.1 pad_maximum_fusion.refs_0_
  11.4 5.9 %all-to-all-start = ((bf16[16,128,512]{2,1,0:T(8,128)(2,1)}), bf16[16,128,512]{2,1,0:T(8,128)(2,1)S(1)}, u32[]{:S(2)}, u32[]{:S(2)}) async-start(bf16[16,128,512]{2,1,0:T(8,128)(2,1)} %copy-done), calls=%async_computation | async-start | bytes 4194304 | tf_op jit(solution)/shard_map/all_to_all | solution.py:222
  17.3 2.6 %collective-permute-start.4 = (bf16[3,512,256]{2,1,0:T(8,128)(2,1)S(1)}, bf16[3,512,256]{2,1,0:T(8,128)(2,1)S(1)}, u32[]{:S(2)}, u32[]{:S(2)}) collective-permute-start(bf16[3,512,256]{2,1,0:T(8,128)(2,1)S(1)} %pad_maximum_fusion.refs_0_), channel_id=1, source_target_pairs={{0,33},{1,32},{32,1},{33,0},{2,35},{3,34},{34,3},{35,2},{4,37},{5,... | collective-permute-start | bytes 2359304 | tf_op jit(solution)/shard_map/ppermute | solution.py:205
  19.9 0.6 collective-permute-start.3
  20.6 16.9 %collective-permute-done.4.refs_2_ = bf16[3,512,256]{2,1,0:T(8,128)(2,1)S(1)} collective-permute-done((bf16[3,512,256]{2,1,0:T(8,128)(2,1)S(1)}, bf16[3,512,256]{2,1,0:T(8,128)(2,1)S(1)}, u32[]{:S(2)}, u32[]{:S(2)}) %collective-permute-start.4) | collective-permute-done | bytes 786464 | tf_op jit(solution)/shard_map/ppermute | solution.py:205
  37.5 1.0 collective-permute-start.5
  38.5 0.9 copy-done.1
  39.4 0.7 slice.15
  40.1 2.6 %collective-permute-start.2 = (bf16[1,512,256]{2,1,0:T(8,128)(2,1)}, bf16[1,512,256]{2,1,0:T(8,128)(2,1)S(1)}, u32[]{:S(2)}, u32[]{:S(2)}) collective-permute-start(bf16[1,512,256]{2,1,0:T(8,128)(2,1)} %slice.15), channel_id=1, source_target_pairs={{0,192},{64,128},{128,64},{192,0},{1,193},{65,129},{129,65},{193,1... | collective-permute-start | bytes 786440 | tf_op jit(solution)/shard_map/ppermute | solution.py:205
  42.7 0.0 collective-permute-done.3.refs_4_
  42.7 0.9 copy-done.3
  43.6 0.0 collective-permute-done.5.refs_6_
  43.6 0.9 copy-done.5
  44.5 0.0 all-to-all-done.mine_ref
  44.5 0.6 shard_map.38
  45.1 1.6 %collective-permute-start.12 = (bf16[4,128,512]{2,1,0:T(8,128)(2,1)S(1)}, bf16[4,128,512]{2,1,0:T(8,128)(2,1)S(1)}, u32[]{:S(2)}, u32[]{:S(2)}) collective-permute-start(bf16[4,128,512]{2,1,0:T(8,128)(2,1)S(1)} %get-tuple-element.30), channel_id=1, source_target_pairs={{0,2},{2,0},{4,6},{6,4},{8,10},{10,8},{12,14},{14,12},{1,3},{3,1},... | collective-permute-start | bytes 1572872 | tf_op jit(solution)/shard_map/ppermute | solution.py:211
  46.7 4.7 %collective-permute-start.13 = (bf16[4,128,512]{2,1,0:T(8,128)(2,1)S(1)}, bf16[4,128,512]{2,1,0:T(8,128)(2,1)S(1)}, u32[]{:S(2)}, u32[]{:S(2)}) collective-permute-start(bf16[4,128,512]{2,1,0:T(8,128)(2,1)S(1)} %get-tuple-element.31), channel_id=1, source_target_pairs={{0,14},{2,4},{4,2},{6,8},{8,6},{10,12},{12,10},{14,0},{1,15},{3,5}... | collective-permute-start | bytes 1572872 | tf_op jit(solution)/shard_map/ppermute | solution.py:211
  51.4 0.0 collective-permute-start.9
  51.4 1.1 %collective-permute-start.10 = (bf16[2,128,512]{2,1,0:T(8,128)(2,1)}, bf16[2,128,512]{2,1,0:T(8,128)(2,1)S(1)}, u32[]{:S(2)}, u32[]{:S(2)}) collective-permute-start(bf16[2,128,512]{2,1,0:T(8,128)(2,1)} %copy-done.8), channel_id=1, source_target_pairs={{0,192},{64,128},{128,64},{192,0},{1,193},{65,129},{129,65},{193,1... | collective-permute-start | bytes 786440 | tf_op jit(solution)/shard_map/ppermute | solution.py:205
  52.4 0.0 collective-permute-done.2.refs_1_
  52.4 3.1 %collective-permute-start.11 = (bf16[2,128,512]{2,1,0:T(8,128)(2,1)}, bf16[2,128,512]{2,1,0:T(8,128)(2,1)S(1)}, u32[]{:S(2)}, u32[]{:S(2)}) collective-permute-start(bf16[2,128,512]{2,1,0:T(8,128)(2,1)} %copy-done.7), channel_id=1, source_target_pairs={{0,32},{32,0},{1,33},{33,1},{2,34},{34,2},{3,35},{35,3},{4,36},{36... | collective-permute-start | bytes 786440 | tf_op jit(solution)/shard_map/ppermute | solution.py:205
  55.5 2.2 %collective-permute-done.9.refs_1_ = bf16[2,128,512]{2,1,0:T(8,128)(2,1)S(1)} collective-permute-done((bf16[2,128,512]{2,1,0:T(8,128)(2,1)}, bf16[2,128,512]{2,1,0:T(8,128)(2,1)S(1)}, u32[]{:S(2)}, u32[]{:S(2)}) %collective-permute-start.9) | collective-permute-done | bytes 262176 | tf_op jit(solution)/shard_map/ppermute | solution.py:205
  57.7 5.3 %collective-permute-start.6 = (bf16[1,512,256]{2,1,0:T(8,128)(2,1)S(1)}, bf16[1,512,256]{2,1,0:T(8,128)(2,1)S(1)}, u32[]{:S(2)}, u32[]{:S(2)}) collective-permute-start(bf16[1,512,256]{2,1,0:T(8,128)(2,1)S(1)} %collective-permute-done.2.refs_1_), channel_id=1, source_target_pairs={{0,33},{1,32},{32,1},{33,0},{2,35},{3,34},{34,3},{35,2},{4,37},{5,... | collective-permute-start | bytes 786440 | tf_op jit(solution)/shard_map/ppermute | solution.py:205
  63.0 0.0 collective-permute-done.10.refs_2_
  63.0 0.0 collective-permute-done.11.refs_3_
  63.0 0.0 collective-permute-done.12.refs_5_
  63.1 0.1 pad_maximum_fusion.1
  63.2 2.0 %collective-permute-start.14 = (bf16[4,128,512]{2,1,0:T(8,128)(2,1)S(1)}, bf16[4,128,512]{2,1,0:T(8,128)(2,1)S(1)}, u32[]{:S(2)}, u32[]{:S(2)}) collective-permute-start(bf16[4,128,512]{2,1,0:T(8,128)(2,1)S(1)} %pad_maximum_fusion.1), channel_id=1, source_target_pairs={{0,16},{16,0},{1,17},{17,1},{2,18},{18,2},{3,19},{19,3},{4,20},{20... | collective-permute-start | bytes 1572872 | tf_op jit(solution)/shard_map/ppermute | solution.py:205
  65.2 0.1 collective-permute-start.7
  65.3 2.7 %collective-permute-done.6.refs_3_ = bf16[1,512,256]{2,1,0:T(8,128)(2,1)S(1)} collective-permute-done((bf16[1,512,256]{2,1,0:T(8,128)(2,1)S(1)}, bf16[1,512,256]{2,1,0:T(8,128)(2,1)S(1)}, u32[]{:S(2)}, u32[]{:S(2)}) %collective-permute-start.6) | collective-permute-done | bytes 262176 | tf_op jit(solution)/shard_map/ppermute | solution.py:205
  68.0 2.3 %collective-permute-start.8 = (bf16[1,512,256]{2,1,0:T(8,128)(2,1)S(1)}, bf16[1,512,256]{2,1,0:T(8,128)(2,1)S(1)}, u32[]{:S(2)}, u32[]{:S(2)}) collective-permute-start(bf16[1,512,256]{2,1,0:T(8,128)(2,1)S(1)} %collective-permute-done.6.refs_3_), channel_id=1, source_target_pairs={{0,16},{16,0},{1,17},{17,1},{2,18},{18,2},{3,19},{19,3},{4,20},{20... | collective-permute-start | bytes 786440 | tf_op jit(solution)/shard_map/ppermute | solution.py:205
  70.3 0.0 collective-permute-done.7.refs_5_
  70.3 1.2 %collective-permute-done.8.refs_7_ = bf16[1,512,256]{2,1,0:T(8,128)(2,1)S(1)} collective-permute-done((bf16[1,512,256]{2,1,0:T(8,128)(2,1)S(1)}, bf16[1,512,256]{2,1,0:T(8,128)(2,1)S(1)}, u32[]{:S(2)}, u32[]{:S(2)}) %collective-permute-start.8) | collective-permute-done | bytes 262176 | tf_op jit(solution)/shard_map/ppermute | solution.py:205
  71.5 3.0 %shard_map.39 = (f32[512,512]{1,0:T(8,128)S(1)}, bf16[512,2048]{1,0:T(8,128)(2,1)S(1)}) custom-call(s32[1,3]{1,0:T(1,128)S(1)} %add_bitcast_fusion.place_ref, bf16[16,128,512]{2,1,0:T(8,128)(2,1)S(1)} %all-to-all-done.mine_ref, bf16[3,512,256]{2,1,0:T(8,128)(2,1)S(1)} %pad_maximum_fusion.refs_0_, bf16[1,512,256]{2,1,0:T(8,128)(2,1)S(1)} %collective-permute-done.2.refs_1_, ...), custom_call_target="tpu_custom_call" | custom-call | tf_op jit(solution)/shard_map/pallas_call | solution.py:114
  74.5 0.0 collective-permute-done.14.refs_4_
  74.5 5.4 %shard_map.40 = (f32[512,512]{1,0:T(8,128)S(1)}, f32[256,1,128]{2,1,0:T(1,128)S(1)}) custom-call(s32[1,3]{1,0:T(1,128)S(1)} %add_bitcast_fusion.place_ref, f32[512,512]{1,0:T(8,128)S(1)} %get-tuple-element.33.partial_ref, bf16[512,2048]{1,0:T(8,128)(2,1)S(1)} %get-tuple-element.34.rest_ref, bf16[2,128,512]{2,1,0:T(8,128)(2,1)S(1)} %get-tuple-element.35.refs_0_, ...), custom_call_target="tpu_custom_call" | custom-call | tf_op jit(solution)/shard_map/pallas_call | solution.py:169
  79.8 22.6 %all_to_all.10.sums_ref = f32[256,1,128]{2,1,0:T(1,128)S(1)} all-to-all(f32[256,1,128]{2,1,0:T(1,128)S(1)} %get-tuple-element.45), channel_id=1, replica_groups=mesh['x'=4,'yl'=2,'core'=2,'prec'=8,'pair'=2] {'x','yl','core','prec','p..., dimensions={0} | all-to-all | bytes 262144 | tf_op jit(solution)/shard_map/all_to_all | solution.py:243
  102.4 1.5 %shard_map.41 = f32[512,512]{1,0:T(8,128)} custom-call(f32[256,1,128]{2,1,0:T(1,128)S(1)} %all_to_all.10.sums_ref, f32[512,512]{1,0:T(8,128)S(1)} %get-tuple-element.46.update_ref), custom_call_target="tpu_custom_call" | custom-call | tf_op jit(solution)/shard_map/pallas_call | solution.py:192
  (19 shorter events, 0.1 us)
Async XLA Ops:
  1.1 9.6 %collective-permute-start.1 = (bf16[512,256]{1,0:T(8,128)(2,1)S(1)}, bf16[512,256]{1,0:T(8,128)(2,1)S(1)}, u32[]{:S(2)}, u32[]{:S(2)}) collective-permute-start(bf16[512,256]{1,0:T(8,128)(2,1)S(1)} %bitcast.11), channel_id=1, source_target_pairs={{0,192},{64,128},{128,64},{192,0},{1,193},{65,129},{129,65},{193,1... | collective-permute-start | bytes 786440 | tf_op jit(solution)/shard_map/ppermute | solution.py:205
  4.5 6.9 %collective-permute-start = (bf16[512,256]{1,0:T(8,128)(2,1)S(1)}, bf16[512,256]{1,0:T(8,128)(2,1)S(1)}, u32[]{:S(2)}, u32[]{:S(2)}) collective-permute-start(bf16[512,256]{1,0:T(8,128)(2,1)S(1)} %bitcast.12), channel_id=1, source_target_pairs={{0,64},{64,0},{128,192},{192,128},{1,65},{65,1},{129,193},{193,129... | collective-permute-start | bytes 786440 | tf_op jit(solution)/shard_map/ppermute | solution.py:205
  7.9 1.4 %copy-start = (bf16[16,128,512]{2,1,0:T(8,128)(2,1)}, bf16[16,128,512]{2,1,0:T(8,128)(2,1)S(1)}, u32[]{:S(2)}) copy-start(bf16[16,128,512]{2,1,0:T(8,128)(2,1)S(1)} %get-tuple-element.27) | copy-start | bytes 6291460
  9.3 0.7 copy-start.7
  10.0 0.7 copy-start.9
  10.7 0.8 copy-start.8
  11.4 33.1 %all-to-all-start = ((bf16[16,128,512]{2,1,0:T(8,128)(2,1)}), bf16[16,128,512]{2,1,0:T(8,128)(2,1)S(1)}, u32[]{:S(2)}, u32[]{:S(2)}) async-start(bf16[16,128,512]{2,1,0:T(8,128)(2,1)} %copy-done), calls=%async_computation | async-start | bytes 4194304 | tf_op jit(solution)/shard_map/all_to_all | solution.py:222
  17.3 20.2 %collective-permute-start.4 = (bf16[3,512,256]{2,1,0:T(8,128)(2,1)S(1)}, bf16[3,512,256]{2,1,0:T(8,128)(2,1)S(1)}, u32[]{:S(2)}, u32[]{:S(2)}) collective-permute-start(bf16[3,512,256]{2,1,0:T(8,128)(2,1)S(1)} %pad_maximum_fusion.refs_0_), channel_id=1, source_target_pairs={{0,33},{1,32},{32,1},{33,0},{2,35},{3,34},{34,3},{35,2},{4,37},{5,... | collective-permute-start | bytes 2359304 | tf_op jit(solution)/shard_map/ppermute | solution.py:205
  19.9 22.8 %collective-permute-start.3 = (bf16[3,512,256]{2,1,0:T(8,128)(2,1)S(1)}, bf16[3,512,256]{2,1,0:T(8,128)(2,1)S(1)}, u32[]{:S(2)}, u32[]{:S(2)}) collective-permute-start(bf16[3,512,256]{2,1,0:T(8,128)(2,1)S(1)} %pad_maximum_fusion.refs_0_), channel_id=1, source_target_pairs={{0,16},{16,0},{1,17},{17,1},{2,18},{18,2},{3,19},{19,3},{4,20},{20... | collective-permute-start | bytes 2359304 | tf_op jit(solution)/shard_map/ppermute | solution.py:205
  37.5 6.1 %collective-permute-start.5 = (bf16[3,512,256]{2,1,0:T(8,128)(2,1)S(1)}, bf16[3,512,256]{2,1,0:T(8,128)(2,1)S(1)}, u32[]{:S(2)}, u32[]{:S(2)}) collective-permute-start(bf16[3,512,256]{2,1,0:T(8,128)(2,1)S(1)} %collective-permute-done.4.refs_2_), channel_id=1, source_target_pairs={{0,16},{16,0},{1,17},{17,1},{2,18},{18,2},{3,19},{19,3},{4,20},{20... | collective-permute-start | bytes 2359304 | tf_op jit(solution)/shard_map/ppermute | solution.py:205
  38.5 0.9 copy-start.1
  40.1 12.3 %collective-permute-start.2 = (bf16[1,512,256]{2,1,0:T(8,128)(2,1)}, bf16[1,512,256]{2,1,0:T(8,128)(2,1)S(1)}, u32[]{:S(2)}, u32[]{:S(2)}) collective-permute-start(bf16[1,512,256]{2,1,0:T(8,128)(2,1)} %slice.15), channel_id=1, source_target_pairs={{0,192},{64,128},{128,64},{192,0},{1,193},{65,129},{129,65},{193,1... | collective-permute-start | bytes 786440 | tf_op jit(solution)/shard_map/ppermute | solution.py:205
  42.7 0.9 copy-start.3
  43.6 0.9 copy-start.5
  44.5 27.0 %copy-start.2 = (bf16[3,512,256]{2,1,0:T(8,128)(2,1)S(1)}, bf16[3,512,256]{2,1,0:T(8,128)(2,1)}, u32[]{:S(2)}) copy-start(bf16[3,512,256]{2,1,0:T(8,128)(2,1)} %copy-done.1) | copy-start | bytes 2359300
  44.5 27.0 %copy-start.4 = (bf16[3,512,256]{2,1,0:T(8,128)(2,1)S(1)}, bf16[3,512,256]{2,1,0:T(8,128)(2,1)}, u32[]{:S(2)}) copy-start(bf16[3,512,256]{2,1,0:T(8,128)(2,1)} %copy-done.3) | copy-start | bytes 2359300
  44.5 27.0 %copy-start.6 = (bf16[3,512,256]{2,1,0:T(8,128)(2,1)S(1)}, bf16[3,512,256]{2,1,0:T(8,128)(2,1)}, u32[]{:S(2)}) copy-start(bf16[3,512,256]{2,1,0:T(8,128)(2,1)} %copy-done.5) | copy-start | bytes 2359300
  45.1 17.9 %collective-permute-start.12 = (bf16[4,128,512]{2,1,0:T(8,128)(2,1)S(1)}, bf16[4,128,512]{2,1,0:T(8,128)(2,1)S(1)}, u32[]{:S(2)}, u32[]{:S(2)}) collective-permute-start(bf16[4,128,512]{2,1,0:T(8,128)(2,1)S(1)} %get-tuple-element.30), channel_id=1, source_target_pairs={{0,2},{2,0},{4,6},{6,4},{8,10},{10,8},{12,14},{14,12},{1,3},{3,1},... | collective-permute-start | bytes 1572872 | tf_op jit(solution)/shard_map/ppermute | solution.py:211
  46.7 16.4 %collective-permute-start.13 = (bf16[4,128,512]{2,1,0:T(8,128)(2,1)S(1)}, bf16[4,128,512]{2,1,0:T(8,128)(2,1)S(1)}, u32[]{:S(2)}, u32[]{:S(2)}) collective-permute-start(bf16[4,128,512]{2,1,0:T(8,128)(2,1)S(1)} %get-tuple-element.31), channel_id=1, source_target_pairs={{0,14},{2,4},{4,2},{6,8},{8,6},{10,12},{12,10},{14,0},{1,15},{3,5}... | collective-permute-start | bytes 1572872 | tf_op jit(solution)/shard_map/ppermute | solution.py:211
  51.4 6.4 %collective-permute-start.9 = (bf16[2,128,512]{2,1,0:T(8,128)(2,1)}, bf16[2,128,512]{2,1,0:T(8,128)(2,1)S(1)}, u32[]{:S(2)}, u32[]{:S(2)}) collective-permute-start(bf16[2,128,512]{2,1,0:T(8,128)(2,1)} %copy-done.9), channel_id=1, source_target_pairs={{0,64},{64,0},{128,192},{192,128},{1,65},{65,1},{129,193},{193,129... | collective-permute-start | bytes 786440 | tf_op jit(solution)/shard_map/ppermute | solution.py:205
  51.4 11.7 %collective-permute-start.10 = (bf16[2,128,512]{2,1,0:T(8,128)(2,1)}, bf16[2,128,512]{2,1,0:T(8,128)(2,1)S(1)}, u32[]{:S(2)}, u32[]{:S(2)}) collective-permute-start(bf16[2,128,512]{2,1,0:T(8,128)(2,1)} %copy-done.8), channel_id=1, source_target_pairs={{0,192},{64,128},{128,64},{192,0},{1,193},{65,129},{129,65},{193,1... | collective-permute-start | bytes 786440 | tf_op jit(solution)/shard_map/ppermute | solution.py:205
  52.4 10.6 %collective-permute-start.11 = (bf16[2,128,512]{2,1,0:T(8,128)(2,1)}, bf16[2,128,512]{2,1,0:T(8,128)(2,1)S(1)}, u32[]{:S(2)}, u32[]{:S(2)}) collective-permute-start(bf16[2,128,512]{2,1,0:T(8,128)(2,1)} %copy-done.7), channel_id=1, source_target_pairs={{0,32},{32,0},{1,33},{33,1},{2,34},{34,2},{3,35},{35,3},{4,36},{36... | collective-permute-start | bytes 786440 | tf_op jit(solution)/shard_map/ppermute | solution.py:205
  57.7 10.2 %collective-permute-start.6 = (bf16[1,512,256]{2,1,0:T(8,128)(2,1)S(1)}, bf16[1,512,256]{2,1,0:T(8,128)(2,1)S(1)}, u32[]{:S(2)}, u32[]{:S(2)}) collective-permute-start(bf16[1,512,256]{2,1,0:T(8,128)(2,1)S(1)} %collective-permute-done.2.refs_1_), channel_id=1, source_target_pairs={{0,33},{1,32},{32,1},{33,0},{2,35},{3,34},{34,3},{35,2},{4,37},{5,... | collective-permute-start | bytes 786440 | tf_op jit(solution)/shard_map/ppermute | solution.py:205
  63.2 11.3 %collective-permute-start.14 = (bf16[4,128,512]{2,1,0:T(8,128)(2,1)S(1)}, bf16[4,128,512]{2,1,0:T(8,128)(2,1)S(1)}, u32[]{:S(2)}, u32[]{:S(2)}) collective-permute-start(bf16[4,128,512]{2,1,0:T(8,128)(2,1)S(1)} %pad_maximum_fusion.1), channel_id=1, source_target_pairs={{0,16},{16,0},{1,17},{17,1},{2,18},{18,2},{3,19},{19,3},{4,20},{20... | collective-permute-start | bytes 1572872 | tf_op jit(solution)/shard_map/ppermute | solution.py:205
  65.2 5.1 %collective-permute-start.7 = (bf16[1,512,256]{2,1,0:T(8,128)(2,1)S(1)}, bf16[1,512,256]{2,1,0:T(8,128)(2,1)S(1)}, u32[]{:S(2)}, u32[]{:S(2)}) collective-permute-start(bf16[1,512,256]{2,1,0:T(8,128)(2,1)S(1)} %collective-permute-done.2.refs_1_), channel_id=1, source_target_pairs={{0,16},{16,0},{1,17},{17,1},{2,18},{18,2},{3,19},{19,3},{4,20},{20... | collective-permute-start | bytes 786440 | tf_op jit(solution)/shard_map/ppermute | solution.py:205
  68.0 3.5 %collective-permute-start.8 = (bf16[1,512,256]{2,1,0:T(8,128)(2,1)S(1)}, bf16[1,512,256]{2,1,0:T(8,128)(2,1)S(1)}, u32[]{:S(2)}, u32[]{:S(2)}) collective-permute-start(bf16[1,512,256]{2,1,0:T(8,128)(2,1)S(1)} %collective-permute-done.6.refs_3_), channel_id=1, source_target_pairs={{0,16},{16,0},{1,17},{17,1},{2,18},{18,2},{3,19},{19,3},{4,20},{20... | collective-permute-start | bytes 786440 | tf_op jit(solution)/shard_map/ppermute | solution.py:205

commit v4 on v3

--- a/solution.py
+++ b/solution.py
@@ -19,10 +19,9 @@
 HALF = 128
 NEAR = (0, 4, 12, 2)
 FAR = ((8, 9, 6, 7), (10, 11, 14, 15))
-ORDER = NEAR + tuple(bits + 1 for bits in NEAR) + FAR[0] + FAR[1]
-GROUPS = tuple(
-    tuple(4 * x + offset for x in some) for offset in (0, 2, 1, 3) for some in ((0, 1, 3), (2,))
-)
+LATE = (8, 10, 9, 11)
+ORDER = NEAR + tuple(bits + 1 for bits in NEAR) + FAR[0][2:] + FAR[1][2:]
+GROUPS = tuple(tuple(4 * x + offset for x in (0, 1, 3)) for offset in (0, 2, 1, 3))
 
 
 def dot(left, right, contract=ROWS_BY_COLUMNS):
@@ -101,16 +100,16 @@
     theirs = pl.ds(pl.multiple_of((1 - odd) * HALF, HALF), HALF)
     for group, group_ref in enumerate(acts):
         for slot, bits in enumerate(GROUPS[group]):
-            columns = pl.ds(pl.multiple_of((shard ^ bits) * HALF, HALF), HALF)
+            columns = pl.ds(ORDER.index(bits) * HALF, HALF)
             acts_ref[:, columns] = group_ref[slot, :, mine]
-            rest_ref[:, pl.ds(ORDER.index(bits) * HALF, HALF)] = group_ref[slot, :, theirs]
-    shards = mine_ref.shape[0]
-    partial_ref[...] = dot(acts_ref[...], mine_ref[...].reshape(shards * HALF, BLK))
+            rest_ref[:, columns] = group_ref[slot, :, theirs]
+    blocks = jnp.concatenate([mine_ref[shard ^ bits] for bits in ORDER], axis=0)
+    partial_ref[...] = dot(acts_ref[...], blocks)
 
 
 def half_gradient(place, mine, acts):
     vmem = pl.BlockSpec(memory_space=pltpu.VMEM)
-    tokens = mine.shape[0] * HALF
+    tokens = len(ORDER) * HALF
     return pl.pallas_call(
         half_step,
         out_shape=(
@@ -125,10 +124,19 @@
 
 
 def block_step(place_ref, partial_ref, rest_ref, *refs):
-    near, others, (update_ref, sums_ref, root_ref) = refs[: len(NEAR)], refs[len(NEAR) : -3], refs[-3:]
+    late, mine, (first_ref, second_ref, taken_ref) = refs[:4], refs[4:6], refs[6:9]
+    near, (update_ref, sums_ref, root_ref) = refs[9:-3], refs[-3:]
+    odd = place_ref[0, 2] == 1
+    transposed = partial_ref[...]
+    for act_ref, bits in zip(late, LATE, strict=True):
+        part = bits // 2 % 2
+        own = mine[part][bits % 2]
+        other = (first_ref, second_ref)[part][bits % 2]
+        piece = [jnp.where(odd, other, own), jnp.where(odd, own, other)]
+        transposed = transposed + dot(act_ref[0], jnp.concatenate(piece, axis=0))
     pieces = [jnp.concatenate([near_ref[0] for near_ref in near], axis=0)]
-    pieces += [other_ref[...].reshape(-1, BLK) for other_ref in others]
-    transposed = partial_ref[...]
+    pieces += [taken_ref[...].reshape(-1, BLK)]
+    pieces += [jnp.concatenate([ref[2], ref[3]], axis=0) for ref in (first_ref, second_ref)]
     start = 0
     for piece in pieces:
         transposed = transposed + dot(rest_ref[:, start : start + piece.shape[0]], piece)
@@ -229,17 +237,19 @@
     ways = (("x", 1), ("x", 3), ("yl", 1))
     near_grads, _ = lax.optimization_barrier((near_grads, (first, second)))
     near_grads = [swap(value, (axis,), bits) for value, (axis, bits) in zip(near_grads, ways, strict=True)]
+    picked = first, second
     first, second = swap_planes(first, True), swap_planes(second, False)
     last_y = swap(last, ("yl", "pair"), 3)
     far_last = [swap(value, ("core",), 1) for value in (last, last_y)]
-    acts = [three, last, three_y, last_y, far_three[0], far_last[0], far_three[1], far_last[1]]
+    acts = [three, three_y, *far_three]
+    late = [last, last_y, *far_last]
     near_grads, _ = lax.optimization_barrier((near_grads, (first, second)))
     near_grads = [here] + near_grads
     taken = swap(jnp.stack([value[1] for value in near_grads]), ("core",), 1)
     partial, rest = half_gradient(place, mine, acts)
 
     devices = 256
-    update, sums = run_block(place, partial, rest, (*near_grads, taken, first, second), devices)
+    update, sums = run_block(place, partial, rest, (*late, *picked, first, second, taken, *near_grads), devices)
     sums = lax.all_to_all(sums, EVERY, 0, 0, tiled=True)
     return graft(sums, update)
 

time: 104 us -> 101 us (0.971)
  waiting for transfers between devices: 23.6 us -> 22.5 us
    pallas_call x1, Pallas kernels: 3 us -> 1.8 us  [half_gradient(): pl.pallas_call(half_step, out_shape=(jax.ShapeDtypeStruct((BLK, BLK), jnp...]
    ppermute x13, waiting for transfers between devices: 23.6 us -> 22.5 us  [swap(): return lax.ppermute(value, axes, [(i, i ^ bits) for i in range(size)])]
  transfers between devices with their start and end apart: 16 -> 16, of which waited for: 5 -> 4; matrix products, arithmetic and copies ran while one was open for 1% -> 1% of each run, Pallas kernels for 6% -> 5%
where the time goes in v4:
time: 101 us
  starting transfers between devices  36.2 us (36%)
  waiting for transfers between devices  22.5 us (22%)
  blocking collectives  21.7 us (21%)
  Pallas kernels  12.4 us (12%)
  local copies, waits for them, and re-layouts  7.29 us (7%)
    ppermute x13, starting transfers between devices, swap(): return lax.ppermute(value, axes, [(i, i ^ bits) for i in range(size)])  24.1 us
    ppermute x13, waiting for transfers between devices, swap(): return lax.ppermute(value, axes, [(i, i ^ bits) for i in range(size)])  22.5 us
    all_to_all x1, blocking collectives, per_device(): sums = lax.all_to_all(sums, EVERY, 0, 0, tiled=True)  21.7 us
    unnamed x21, local copies, waits for them, and re-layouts  6.51 us
    ppermute x2, starting transfers between devices, swap_planes(): return lax.ppermute(value, 'prec', pairs)  6.23 us
    all_to_all x1, starting transfers between devices, per_device(): mine = lax.all_to_all(mine, DP, 0, 0, tiled=True)  5.87 us
    pallas_call x1, Pallas kernels, run_block(): pl.pallas_call(block_step, out_shape=(jax.ShapeDtypeStruct((BLK, BLK), jn...  5.83 us
    pallas_call x1, Pallas kernels, cut(): pl.pallas_call(cut_step, out_shape=[jax.ShapeDtypeStruct((shards, HALF, B...  2.69 us
  transfers between devices with their start and end apart: 16, of which 4 were waited for; matrix products, arithmetic and copies ran while one was open for 1% of the time, Pallas kernels for 5%

profile of v4, /device:TPU:1, one launch (start us, length us, event | category | flops | bytes accessed | tf_op | source)
XLA Modules:
  0.0 101.1 jit_solution(9755505887188628391)
XLA Ops:
  0.0 1.1 %copy.4 = bf16[256,512]{0,1:T(8,128)(2,1)S(1)} copy(bf16[256,512]{1,0:T(8,128)(2,1)} %param.3) | data formatting | bytes 524288 | tf_op args[0]
  1.1 3.4 %collective-permute-start.1 = (bf16[512,256]{1,0:T(8,128)(2,1)S(1)}, bf16[512,256]{1,0:T(8,128)(2,1)S(1)}, u32[]{:S(2)}, u32[]{:S(2)}) collective-permute-start(bf16[512,256]{1,0:T(8,128)(2,1)S(1)} %bitcast.11), channel_id=1, source_target_pairs={{0,192},{64,128},{128,64},{192,0},{1,193},{65,129},{129,65},{193,1... | collective-permute-start | bytes 786440 | tf_op jit(solution)/shard_map/ppermute | solution.py:213
  4.5 0.0 collective-permute-start
  5.1 0.1 add_bitcast_fusion.place_ref
  5.2 2.7 %shard_map.37 = (bf16[16,128,512]{2,1,0:T(8,128)(2,1)S(1)}, bf16[2,128,512]{2,1,0:T(8,128)(2,1)S(1)}, bf16[2,128,512]{2,1,0:T(8,128)(2,1)S(1)}, bf16[2,128,512]{2,1,0:T(8,128)(2,1)S(1)}, bf16[2,128,512]{2,1,0:T(8,128)(2,1)S(1)}) custom-call(s32[1,3]{1,0:T(1,128)S(1)} %add_bitcast_fusion.place_ref, bf16[256,8192]{1,0:T(8,128)(2,1)} %grads_ref.1), custom_call_target="tpu_custom_call" | custom-call | tf_op jit(solution)/shard_map/pallas_call | solution.py:68
  7.9 1.3 %copy-done = bf16[16,128,512]{2,1,0:T(8,128)(2,1)} copy-done((bf16[16,128,512]{2,1,0:T(8,128)(2,1)}, bf16[16,128,512]{2,1,0:T(8,128)(2,1)S(1)}, u32[]{:S(2)}) %copy-start) | copy-done | bytes 2097176
  9.3 0.7 copy-done.7
  10.0 0.7 copy-done.9
  10.7 0.0 collective-permute-done.1
  10.7 0.7 collective-permute-done
  11.3 0.1 pad_maximum_fusion.refs_0_
  11.4 5.9 %all-to-all-start = ((bf16[16,128,512]{2,1,0:T(8,128)(2,1)}), bf16[16,128,512]{2,1,0:T(8,128)(2,1)S(1)}, u32[]{:S(2)}, u32[]{:S(2)}) async-start(bf16[16,128,512]{2,1,0:T(8,128)(2,1)} %copy-done), calls=%async_computation | async-start | bytes 4194304 | tf_op jit(solution)/shard_map/all_to_all | solution.py:230
  17.3 2.6 %collective-permute-start.2 = (bf16[3,512,256]{2,1,0:T(8,128)(2,1)S(1)}, bf16[3,512,256]{2,1,0:T(8,128)(2,1)S(1)}, u32[]{:S(2)}, u32[]{:S(2)}) collective-permute-start(bf16[3,512,256]{2,1,0:T(8,128)(2,1)S(1)} %pad_maximum_fusion.refs_0_), channel_id=1, source_target_pairs={{0,33},{1,32},{32,1},{33,0},{2,35},{3,34},{34,3},{35,2},{4,37},{5,... | collective-permute-start | bytes 2359304 | tf_op jit(solution)/shard_map/ppermute | solution.py:213
  19.9 0.6 collective-permute-start.3
  20.6 16.9 %collective-permute-done.2.refs_1_ = bf16[3,512,256]{2,1,0:T(8,128)(2,1)S(1)} collective-permute-done((bf16[3,512,256]{2,1,0:T(8,128)(2,1)S(1)}, bf16[3,512,256]{2,1,0:T(8,128)(2,1)S(1)}, u32[]{:S(2)}, u32[]{:S(2)}) %collective-permute-start.2) | collective-permute-done | bytes 786464 | tf_op jit(solution)/shard_map/ppermute | solution.py:213
  37.5 1.0 collective-permute-start.4
  38.5 0.9 copy-done.1
  39.4 0.7 slice.15
  40.1 2.6 %collective-permute-start.5 = (bf16[1,512,256]{2,1,0:T(8,128)(2,1)}, bf16[1,512,256]{2,1,0:T(8,128)(2,1)S(1)}, u32[]{:S(2)}, u32[]{:S(2)}) collective-permute-start(bf16[1,512,256]{2,1,0:T(8,128)(2,1)} %slice.15), channel_id=1, source_target_pairs={{0,192},{64,128},{128,64},{192,0},{1,193},{65,129},{129,65},{193,1... | collective-permute-start | bytes 786440 | tf_op jit(solution)/shard_map/ppermute | solution.py:213
  42.7 0.0 collective-permute-done.3.refs_2_
  42.7 0.9 copy-done.3
  43.6 0.0 collective-permute-done.4.refs_3_
  43.6 0.9 copy-done.5
  44.5 0.0 all-to-all-done.mine_ref
  44.5 0.6 shard_map.39
  45.1 1.6 %collective-permute-start.9 = (bf16[4,128,512]{2,1,0:T(8,128)(2,1)S(1)}, bf16[4,128,512]{2,1,0:T(8,128)(2,1)S(1)}, u32[]{:S(2)}, u32[]{:S(2)}) collective-permute-start(bf16[4,128,512]{2,1,0:T(8,128)(2,1)S(1)} %get-tuple-element.32.refs_4_), channel_id=1, source_target_pairs={{0,2},{2,0},{4,6},{6,4},{8,10},{10,8},{12,14},{14,12},{1,3},{3,1},... | collective-permute-start | bytes 1572872 | tf_op jit(solution)/shard_map/ppermute | solution.py:219
  46.7 4.7 %collective-permute-start.10 = (bf16[4,128,512]{2,1,0:T(8,128)(2,1)S(1)}, bf16[4,128,512]{2,1,0:T(8,128)(2,1)S(1)}, u32[]{:S(2)}, u32[]{:S(2)}) collective-permute-start(bf16[4,128,512]{2,1,0:T(8,128)(2,1)S(1)} %get-tuple-element.33.refs_5_), channel_id=1, source_target_pairs={{0,14},{2,4},{4,2},{6,8},{8,6},{10,12},{12,10},{14,0},{1,15},{3,5}... | collective-permute-start | bytes 1572872 | tf_op jit(solution)/shard_map/ppermute | solution.py:219
  51.4 0.0 collective-permute-start.11
  51.4 1.1 %collective-permute-start.12 = (bf16[2,128,512]{2,1,0:T(8,128)(2,1)}, bf16[2,128,512]{2,1,0:T(8,128)(2,1)S(1)}, u32[]{:S(2)}, u32[]{:S(2)}) collective-permute-start(bf16[2,128,512]{2,1,0:T(8,128)(2,1)} %copy-done.8), channel_id=1, source_target_pairs={{0,192},{64,128},{128,64},{192,0},{1,193},{65,129},{129,65},{193,1... | collective-permute-start | bytes 786440 | tf_op jit(solution)/shard_map/ppermute | solution.py:213
  52.4 0.0 collective-permute-done.5.refs_0_
  52.4 3.1 %collective-permute-start.13 = (bf16[2,128,512]{2,1,0:T(8,128)(2,1)}, bf16[2,128,512]{2,1,0:T(8,128)(2,1)S(1)}, u32[]{:S(2)}, u32[]{:S(2)}) collective-permute-start(bf16[2,128,512]{2,1,0:T(8,128)(2,1)} %copy-done.7), channel_id=1, source_target_pairs={{0,32},{32,0},{1,33},{33,1},{2,34},{34,2},{3,35},{35,3},{4,36},{36... | collective-permute-start | bytes 786440 | tf_op jit(solution)/shard_map/ppermute | solution.py:213
  55.5 2.2 %collective-permute-done.11.refs_10_ = bf16[2,128,512]{2,1,0:T(8,128)(2,1)S(1)} collective-permute-done((bf16[2,128,512]{2,1,0:T(8,128)(2,1)}, bf16[2,128,512]{2,1,0:T(8,128)(2,1)S(1)}, u32[]{:S(2)}, u32[]{:S(2)}) %collective-permute-start.11) | collective-permute-done | bytes 262176 | tf_op jit(solution)/shard_map/ppermute | solution.py:213
  57.7 5.3 %collective-permute-start.6 = (bf16[1,512,256]{2,1,0:T(8,128)(2,1)S(1)}, bf16[1,512,256]{2,1,0:T(8,128)(2,1)S(1)}, u32[]{:S(2)}, u32[]{:S(2)}) collective-permute-start(bf16[1,512,256]{2,1,0:T(8,128)(2,1)S(1)} %collective-permute-done.5.refs_0_), channel_id=1, source_target_pairs={{0,33},{1,32},{32,1},{33,0},{2,35},{3,34},{34,3},{35,2},{4,37},{5,... | collective-permute-start | bytes 786440 | tf_op jit(solution)/shard_map/ppermute | solution.py:213
  63.0 0.0 collective-permute-done.12.refs_11_
  63.0 0.0 collective-permute-done.13.refs_12_
  63.0 0.0 collective-permute-done.9.refs_6_
  63.0 0.0 collective-permute-done.10.refs_7_
  63.1 0.1 pad_maximum_fusion.1
  63.2 2.0 %collective-permute-start.14 = (bf16[4,128,512]{2,1,0:T(8,128)(2,1)S(1)}, bf16[4,128,512]{2,1,0:T(8,128)(2,1)S(1)}, u32[]{:S(2)}, u32[]{:S(2)}) collective-permute-start(bf16[4,128,512]{2,1,0:T(8,128)(2,1)S(1)} %pad_maximum_fusion.1), channel_id=1, source_target_pairs={{0,16},{16,0},{1,17},{17,1},{2,18},{18,2},{3,19},{19,3},{4,20},{20... | collective-permute-start | bytes 1572872 | tf_op jit(solution)/shard_map/ppermute | solution.py:213
  65.2 0.1 collective-permute-start.7
  65.3 2.7 %collective-permute-done.6.refs_1_ = bf16[1,512,256]{2,1,0:T(8,128)(2,1)S(1)} collective-permute-done((bf16[1,512,256]{2,1,0:T(8,128)(2,1)S(1)}, bf16[1,512,256]{2,1,0:T(8,128)(2,1)S(1)}, u32[]{:S(2)}, u32[]{:S(2)}) %collective-permute-start.6) | collective-permute-done | bytes 262176 | tf_op jit(solution)/shard_map/ppermute | solution.py:213
  68.0 2.3 %collective-permute-start.8 = (bf16[1,512,256]{2,1,0:T(8,128)(2,1)S(1)}, bf16[1,512,256]{2,1,0:T(8,128)(2,1)S(1)}, u32[]{:S(2)}, u32[]{:S(2)}) collective-permute-start(bf16[1,512,256]{2,1,0:T(8,128)(2,1)S(1)} %collective-permute-done.6.refs_1_), channel_id=1, source_target_pairs={{0,16},{16,0},{1,17},{17,1},{2,18},{18,2},{3,19},{19,3},{4,20},{20... | collective-permute-start | bytes 786440 | tf_op jit(solution)/shard_map/ppermute | solution.py:213
  70.3 1.8 %shard_map.38 = (f32[512,512]{1,0:T(8,128)S(1)}, bf16[512,1536]{1,0:T(8,128)(2,1)S(1)}) custom-call(s32[1,3]{1,0:T(1,128)S(1)} %add_bitcast_fusion.place_ref, bf16[16,128,512]{2,1,0:T(8,128)(2,1)S(1)} %all-to-all-done.mine_ref, bf16[3,512,256]{2,1,0:T(8,128)(2,1)S(1)} %pad_maximum_fusion.refs_0_, bf16[3,512,256]{2,1,0:T(8,128)(2,1)S(1)} %copy-done.2, ...), custom_call_target="tpu_custom_call" | custom-call | tf_op jit(solution)/shard_map/pallas_call | solution.py:113
  72.1 0.0 collective-permute-done.8.refs_3_
  72.1 0.0 collective-permute-done.14.refs_8_
  72.1 5.8 %shard_map.40 = (f32[512,512]{1,0:T(8,128)S(1)}, f32[256,1,128]{2,1,0:T(1,128)S(1)}) custom-call(s32[1,3]{1,0:T(1,128)S(1)} %add_bitcast_fusion.place_ref, f32[512,512]{1,0:T(8,128)S(1)} %get-tuple-element.29.partial_ref, bf16[512,1536]{1,0:T(8,128)(2,1)S(1)} %get-tuple-element.30.rest_ref, bf16[1,512,256]{2,1,0:T(8,128)(2,1)S(1)} %collective-permute-done.5.refs_0_, ...), custom_call_target="tpu_custom_call" | custom-call | tf_op jit(solution)/shard_map/pallas_call | solution.py:177
  78.0 21.7 %all_to_all.10.sums_ref = f32[256,1,128]{2,1,0:T(1,128)S(1)} all-to-all(f32[256,1,128]{2,1,0:T(1,128)S(1)} %get-tuple-element.45), channel_id=1, replica_groups=mesh['x'=4,'yl'=2,'core'=2,'prec'=8,'pair'=2] {'x','yl','core','prec','p..., dimensions={0} | all-to-all | bytes 262144 | tf_op jit(solution)/shard_map/all_to_all | solution.py:253
  99.6 1.5 %shard_map.41 = f32[512,512]{1,0:T(8,128)} custom-call(f32[256,1,128]{2,1,0:T(1,128)S(1)} %all_to_all.10.sums_ref, f32[512,512]{1,0:T(8,128)S(1)} %get-tuple-element.46.update_ref), custom_call_target="tpu_custom_call" | custom-call | tf_op jit(solution)/shard_map/pallas_call | solution.py:200
  (19 shorter events, 0.1 us)
Async XLA Ops:
  1.1 9.6 %collective-permute-start.1 = (bf16[512,256]{1,0:T(8,128)(2,1)S(1)}, bf16[512,256]{1,0:T(8,128)(2,1)S(1)}, u32[]{:S(2)}, u32[]{:S(2)}) collective-permute-start(bf16[512,256]{1,0:T(8,128)(2,1)S(1)} %bitcast.11), channel_id=1, source_target_pairs={{0,192},{64,128},{128,64},{192,0},{1,193},{65,129},{129,65},{193,1... | collective-permute-start | bytes 786440 | tf_op jit(solution)/shard_map/ppermute | solution.py:213
  4.5 6.9 %collective-permute-start = (bf16[512,256]{1,0:T(8,128)(2,1)S(1)}, bf16[512,256]{1,0:T(8,128)(2,1)S(1)}, u32[]{:S(2)}, u32[]{:S(2)}) collective-permute-start(bf16[512,256]{1,0:T(8,128)(2,1)S(1)} %bitcast.12), channel_id=1, source_target_pairs={{0,64},{64,0},{128,192},{192,128},{1,65},{65,1},{129,193},{193,129... | collective-permute-start | bytes 786440 | tf_op jit(solution)/shard_map/ppermute | solution.py:213
  7.9 1.4 %copy-start = (bf16[16,128,512]{2,1,0:T(8,128)(2,1)}, bf16[16,128,512]{2,1,0:T(8,128)(2,1)S(1)}, u32[]{:S(2)}) copy-start(bf16[16,128,512]{2,1,0:T(8,128)(2,1)S(1)} %get-tuple-element.27) | copy-start | bytes 6291460
  9.3 0.7 copy-start.7
  10.0 0.7 copy-start.9
  10.7 0.7 copy-start.8
  11.4 33.1 %all-to-all-start = ((bf16[16,128,512]{2,1,0:T(8,128)(2,1)}), bf16[16,128,512]{2,1,0:T(8,128)(2,1)S(1)}, u32[]{:S(2)}, u32[]{:S(2)}) async-start(bf16[16,128,512]{2,1,0:T(8,128)(2,1)} %copy-done), calls=%async_computation | async-start | bytes 4194304 | tf_op jit(solution)/shard_map/all_to_all | solution.py:230
  17.3 20.2 %collective-permute-start.2 = (bf16[3,512,256]{2,1,0:T(8,128)(2,1)S(1)}, bf16[3,512,256]{2,1,0:T(8,128)(2,1)S(1)}, u32[]{:S(2)}, u32[]{:S(2)}) collective-permute-start(bf16[3,512,256]{2,1,0:T(8,128)(2,1)S(1)} %pad_maximum_fusion.refs_0_), channel_id=1, source_target_pairs={{0,33},{1,32},{32,1},{33,0},{2,35},{3,34},{34,3},{35,2},{4,37},{5,... | collective-permute-start | bytes 2359304 | tf_op jit(solution)/shard_map/ppermute | solution.py:213
  19.9 22.8 %collective-permute-start.3 = (bf16[3,512,256]{2,1,0:T(8,128)(2,1)S(1)}, bf16[3,512,256]{2,1,0:T(8,128)(2,1)S(1)}, u32[]{:S(2)}, u32[]{:S(2)}) collective-permute-start(bf16[3,512,256]{2,1,0:T(8,128)(2,1)S(1)} %pad_maximum_fusion.refs_0_), channel_id=1, source_target_pairs={{0,16},{16,0},{1,17},{17,1},{2,18},{18,2},{3,19},{19,3},{4,20},{20... | collective-permute-start | bytes 2359304 | tf_op jit(solution)/shard_map/ppermute | solution.py:213
  37.5 6.1 %collective-permute-start.4 = (bf16[3,512,256]{2,1,0:T(8,128)(2,1)S(1)}, bf16[3,512,256]{2,1,0:T(8,128)(2,1)S(1)}, u32[]{:S(2)}, u32[]{:S(2)}) collective-permute-start(bf16[3,512,256]{2,1,0:T(8,128)(2,1)S(1)} %collective-permute-done.2.refs_1_), channel_id=1, source_target_pairs={{0,16},{16,0},{1,17},{17,1},{2,18},{18,2},{3,19},{19,3},{4,20},{20... | collective-permute-start | bytes 2359304 | tf_op jit(solution)/shard_map/ppermute | solution.py:213
  38.5 0.9 copy-start.1
  40.1 12.3 %collective-permute-start.5 = (bf16[1,512,256]{2,1,0:T(8,128)(2,1)}, bf16[1,512,256]{2,1,0:T(8,128)(2,1)S(1)}, u32[]{:S(2)}, u32[]{:S(2)}) collective-permute-start(bf16[1,512,256]{2,1,0:T(8,128)(2,1)} %slice.15), channel_id=1, source_target_pairs={{0,192},{64,128},{128,64},{192,0},{1,193},{65,129},{129,65},{193,1... | collective-permute-start | bytes 786440 | tf_op jit(solution)/shard_map/ppermute | solution.py:213
  42.7 0.9 copy-start.3
  43.6 0.9 copy-start.5
  44.5 25.8 %copy-start.2 = (bf16[3,512,256]{2,1,0:T(8,128)(2,1)S(1)}, bf16[3,512,256]{2,1,0:T(8,128)(2,1)}, u32[]{:S(2)}) copy-start(bf16[3,512,256]{2,1,0:T(8,128)(2,1)} %copy-done.1) | copy-start | bytes 2359300
  44.5 25.8 %copy-start.4 = (bf16[3,512,256]{2,1,0:T(8,128)(2,1)S(1)}, bf16[3,512,256]{2,1,0:T(8,128)(2,1)}, u32[]{:S(2)}) copy-start(bf16[3,512,256]{2,1,0:T(8,128)(2,1)} %copy-done.3) | copy-start | bytes 2359300
  44.5 25.8 %copy-start.6 = (bf16[3,512,256]{2,1,0:T(8,128)(2,1)S(1)}, bf16[3,512,256]{2,1,0:T(8,128)(2,1)}, u32[]{:S(2)}) copy-start(bf16[3,512,256]{2,1,0:T(8,128)(2,1)} %copy-done.5) | copy-start | bytes 2359300
  45.1 17.9 %collective-permute-start.9 = (bf16[4,128,512]{2,1,0:T(8,128)(2,1)S(1)}, bf16[4,128,512]{2,1,0:T(8,128)(2,1)S(1)}, u32[]{:S(2)}, u32[]{:S(2)}) collective-permute-start(bf16[4,128,512]{2,1,0:T(8,128)(2,1)S(1)} %get-tuple-element.32.refs_4_), channel_id=1, source_target_pairs={{0,2},{2,0},{4,6},{6,4},{8,10},{10,8},{12,14},{14,12},{1,3},{3,1},... | collective-permute-start | bytes 1572872 | tf_op jit(solution)/shard_map/ppermute | solution.py:219
  46.7 16.4 %collective-permute-start.10 = (bf16[4,128,512]{2,1,0:T(8,128)(2,1)S(1)}, bf16[4,128,512]{2,1,0:T(8,128)(2,1)S(1)}, u32[]{:S(2)}, u32[]{:S(2)}) collective-permute-start(bf16[4,128,512]{2,1,0:T(8,128)(2,1)S(1)} %get-tuple-element.33.refs_5_), channel_id=1, source_target_pairs={{0,14},{2,4},{4,2},{6,8},{8,6},{10,12},{12,10},{14,0},{1,15},{3,5}... | collective-permute-start | bytes 1572872 | tf_op jit(solution)/shard_map/ppermute | solution.py:219
  51.4 6.4 %collective-permute-start.11 = (bf16[2,128,512]{2,1,0:T(8,128)(2,1)}, bf16[2,128,512]{2,1,0:T(8,128)(2,1)S(1)}, u32[]{:S(2)}, u32[]{:S(2)}) collective-permute-start(bf16[2,128,512]{2,1,0:T(8,128)(2,1)} %copy-done.9), channel_id=1, source_target_pairs={{0,64},{64,0},{128,192},{192,128},{1,65},{65,1},{129,193},{193,129... | collective-permute-start | bytes 786440 | tf_op jit(solution)/shard_map/ppermute | solution.py:213
  51.4 11.7 %collective-permute-start.12 = (bf16[2,128,512]{2,1,0:T(8,128)(2,1)}, bf16[2,128,512]{2,1,0:T(8,128)(2,1)S(1)}, u32[]{:S(2)}, u32[]{:S(2)}) collective-permute-start(bf16[2,128,512]{2,1,0:T(8,128)(2,1)} %copy-done.8), channel_id=1, source_target_pairs={{0,192},{64,128},{128,64},{192,0},{1,193},{65,129},{129,65},{193,1... | collective-permute-start | bytes 786440 | tf_op jit(solution)/shard_map/ppermute | solution.py:213
  52.4 10.6 %collective-permute-start.13 = (bf16[2,128,512]{2,1,0:T(8,128)(2,1)}, bf16[2,128,512]{2,1,0:T(8,128)(2,1)S(1)}, u32[]{:S(2)}, u32[]{:S(2)}) collective-permute-start(bf16[2,128,512]{2,1,0:T(8,128)(2,1)} %copy-done.7), channel_id=1, source_target_pairs={{0,32},{32,0},{1,33},{33,1},{2,34},{34,2},{3,35},{35,3},{4,36},{36... | collective-permute-start | bytes 786440 | tf_op jit(solution)/shard_map/ppermute | solution.py:213
  57.7 10.2 %collective-permute-start.6 = (bf16[1,512,256]{2,1,0:T(8,128)(2,1)S(1)}, bf16[1,512,256]{2,1,0:T(8,128)(2,1)S(1)}, u32[]{:S(2)}, u32[]{:S(2)}) collective-permute-start(bf16[1,512,256]{2,1,0:T(8,128)(2,1)S(1)} %collective-permute-done.5.refs_0_), channel_id=1, source_target_pairs={{0,33},{1,32},{32,1},{33,0},{2,35},{3,34},{34,3},{35,2},{4,37},{5,... | collective-permute-start | bytes 786440 | tf_op jit(solution)/shard_map/ppermute | solution.py:213
  63.2 8.9 %collective-permute-start.14 = (bf16[4,128,512]{2,1,0:T(8,128)(2,1)S(1)}, bf16[4,128,512]{2,1,0:T(8,128)(2,1)S(1)}, u32[]{:S(2)}, u32[]{:S(2)}) collective-permute-start(bf16[4,128,512]{2,1,0:T(8,128)(2,1)S(1)} %pad_maximum_fusion.1), channel_id=1, source_target_pairs={{0,16},{16,0},{1,17},{17,1},{2,18},{18,2},{3,19},{19,3},{4,20},{20... | collective-permute-start | bytes 1572872 | tf_op jit(solution)/shard_map/ppermute | solution.py:213
  65.2 6.9 %collective-permute-start.7 = (bf16[1,512,256]{2,1,0:T(8,128)(2,1)S(1)}, bf16[1,512,256]{2,1,0:T(8,128)(2,1)S(1)}, u32[]{:S(2)}, u32[]{:S(2)}) collective-permute-start(bf16[1,512,256]{2,1,0:T(8,128)(2,1)S(1)} %collective-permute-done.5.refs_0_), channel_id=1, source_target_pairs={{0,16},{16,0},{1,17},{17,1},{2,18},{18,2},{3,19},{19,3},{4,20},{20... | collective-permute-start | bytes 786440 | tf_op jit(solution)/shard_map/ppermute | solution.py:213
  68.0 4.1 %collective-permute-start.8 = (bf16[1,512,256]{2,1,0:T(8,128)(2,1)S(1)}, bf16[1,512,256]{2,1,0:T(8,128)(2,1)S(1)}, u32[]{:S(2)}, u32[]{:S(2)}) collective-permute-start(bf16[1,512,256]{2,1,0:T(8,128)(2,1)S(1)} %collective-permute-done.6.refs_1_), channel_id=1, source_target_pairs={{0,16},{16,0},{1,17},{17,1},{2,18},{18,2},{3,19},{19,3},{4,20},{20... | collective-permute-start | bytes 786440 | tf_op jit(solution)/shard_map/ppermute | solution.py:213

commit v5 on v4

--- a/solution.py
+++ b/solution.py
@@ -245,8 +245,9 @@
     late = [last, last_y, *far_last]
     near_grads, _ = lax.optimization_barrier((near_grads, (first, second)))
     near_grads = [here] + near_grads
-    taken = swap(jnp.stack([value[1] for value in near_grads]), ("core",), 1)
     partial, rest = half_gradient(place, mine, acts)
+    leaving, _ = lax.optimization_barrier((jnp.stack([value[1] for value in near_grads]), partial))
+    taken = swap(leaving, ("core",), 1)
 
     devices = 256
     update, sums = run_block(place, partial, rest, (*late, *picked, first, second, taken, *near_grads), devices)

time: 101 us -> 101 us (level)
  transfers between devices with their start and end apart: 16 -> 16, of which waited for: 4 -> 5; matrix products, arithmetic and copies ran while one was open for 1% -> 1% of each run, Pallas kernels for 5% -> 5%
where the time goes in v5:
time: 101 us
  starting transfers between devices  36.2 us (36%)
  blocking collectives  22 us (22%)
  waiting for transfers between devices  21.8 us (22%)
  Pallas kernels  12.4 us (12%)
  local copies, waits for them, and re-layouts  7.29 us (7%)
    ppermute x13, starting transfers between devices, swap(): return lax.ppermute(value, axes, [(i, i ^ bits) for i in range(size)])  24.1 us
    all_to_all x1, blocking collectives, per_device(): sums = lax.all_to_all(sums, EVERY, 0, 0, tiled=True)  22 us
    ppermute x13, waiting for transfers between devices, swap(): return lax.ppermute(value, axes, [(i, i ^ bits) for i in range(size)])  21.8 us
    unnamed x21, local copies, waits for them, and re-layouts  6.51 us
    ppermute x2, starting transfers between devices, swap_planes(): return lax.ppermute(value, 'prec', pairs)  6.23 us
    all_to_all x1, starting transfers between devices, per_device(): mine = lax.all_to_all(mine, DP, 0, 0, tiled=True)  5.87 us
    pallas_call x1, Pallas kernels, run_block(): pl.pallas_call(block_step, out_shape=(jax.ShapeDtypeStruct((BLK, BLK), jn...  5.82 us
    pallas_call x1, Pallas kernels, cut(): pl.pallas_call(cut_step, out_shape=[jax.ShapeDtypeStruct((shards, HALF, B...  2.69 us
  transfers between devices with their start and end apart: 16, of which 5 were waited for; matrix products, arithmetic and copies ran while one was open for 1% of the time, Pallas kernels for 5%

profile of v5, /device:TPU:1, one launch (start us, length us, event | category | flops | bytes accessed | tf_op | source)
XLA Modules:
  0.0 100.8 jit_solution(1947955364875031751)
XLA Ops:
  0.0 1.1 %copy.4 = bf16[256,512]{0,1:T(8,128)(2,1)S(1)} copy(bf16[256,512]{1,0:T(8,128)(2,1)} %param.3) | data formatting | bytes 524288 | tf_op args[0]
  1.1 3.4 %collective-permute-start.1 = (bf16[512,256]{1,0:T(8,128)(2,1)S(1)}, bf16[512,256]{1,0:T(8,128)(2,1)S(1)}, u32[]{:S(2)}, u32[]{:S(2)}) collective-permute-start(bf16[512,256]{1,0:T(8,128)(2,1)S(1)} %bitcast.11), channel_id=1, source_target_pairs={{0,192},{64,128},{128,64},{192,0},{1,193},{65,129},{129,65},{193,1... | collective-permute-start | bytes 786440 | tf_op jit(solution)/shard_map/ppermute | solution.py:213
  4.5 0.0 collective-permute-start
  5.1 0.1 add_bitcast_fusion.place_ref
  5.2 2.7 %shard_map.37 = (bf16[16,128,512]{2,1,0:T(8,128)(2,1)S(1)}, bf16[2,128,512]{2,1,0:T(8,128)(2,1)S(1)}, bf16[2,128,512]{2,1,0:T(8,128)(2,1)S(1)}, bf16[2,128,512]{2,1,0:T(8,128)(2,1)S(1)}, bf16[2,128,512]{2,1,0:T(8,128)(2,1)S(1)}) custom-call(s32[1,3]{1,0:T(1,128)S(1)} %add_bitcast_fusion.place_ref, bf16[256,8192]{1,0:T(8,128)(2,1)} %grads_ref.1), custom_call_target="tpu_custom_call" | custom-call | tf_op jit(solution)/shard_map/pallas_call | solution.py:68
  7.9 1.3 %copy-done = bf16[16,128,512]{2,1,0:T(8,128)(2,1)} copy-done((bf16[16,128,512]{2,1,0:T(8,128)(2,1)}, bf16[16,128,512]{2,1,0:T(8,128)(2,1)S(1)}, u32[]{:S(2)}) %copy-start) | copy-done | bytes 2097176
  9.3 0.7 copy-done.7
  10.0 0.7 copy-done.9
  10.7 0.0 collective-permute-done.1
  10.7 0.7 collective-permute-done
  11.3 0.1 pad_maximum_fusion.refs_0_
  11.4 5.9 %all-to-all-start = ((bf16[16,128,512]{2,1,0:T(8,128)(2,1)}), bf16[16,128,512]{2,1,0:T(8,128)(2,1)S(1)}, u32[]{:S(2)}, u32[]{:S(2)}) async-start(bf16[16,128,512]{2,1,0:T(8,128)(2,1)} %copy-done), calls=%async_computation | async-start | bytes 4194304 | tf_op jit(solution)/shard_map/all_to_all | solution.py:230
  17.3 2.6 %collective-permute-start.2 = (bf16[3,512,256]{2,1,0:T(8,128)(2,1)S(1)}, bf16[3,512,256]{2,1,0:T(8,128)(2,1)S(1)}, u32[]{:S(2)}, u32[]{:S(2)}) collective-permute-start(bf16[3,512,256]{2,1,0:T(8,128)(2,1)S(1)} %pad_maximum_fusion.refs_0_), channel_id=1, source_target_pairs={{0,33},{1,32},{32,1},{33,0},{2,35},{3,34},{34,3},{35,2},{4,37},{5,... | collective-permute-start | bytes 2359304 | tf_op jit(solution)/shard_map/ppermute | solution.py:213
  19.9 0.6 collective-permute-start.3
  20.6 16.9 %collective-permute-done.2.refs_1_ = bf16[3,512,256]{2,1,0:T(8,128)(2,1)S(1)} collective-permute-done((bf16[3,512,256]{2,1,0:T(8,128)(2,1)S(1)}, bf16[3,512,256]{2,1,0:T(8,128)(2,1)S(1)}, u32[]{:S(2)}, u32[]{:S(2)}) %collective-permute-start.2) | collective-permute-done | bytes 786464 | tf_op jit(solution)/shard_map/ppermute | solution.py:213
  37.5 1.0 collective-permute-start.4
  38.5 0.9 copy-done.1
  39.4 0.7 slice.15
  40.1 2.6 %collective-permute-start.5 = (bf16[1,512,256]{2,1,0:T(8,128)(2,1)}, bf16[1,512,256]{2,1,0:T(8,128)(2,1)S(1)}, u32[]{:S(2)}, u32[]{:S(2)}) collective-permute-start(bf16[1,512,256]{2,1,0:T(8,128)(2,1)} %slice.15), channel_id=1, source_target_pairs={{0,192},{64,128},{128,64},{192,0},{1,193},{65,129},{129,65},{193,1... | collective-permute-start | bytes 786440 | tf_op jit(solution)/shard_map/ppermute | solution.py:213
  42.7 0.0 collective-permute-done.3.refs_2_
  42.7 0.9 copy-done.3
  43.6 0.0 collective-permute-done.4.refs_3_
  43.6 0.9 copy-done.5
  44.5 0.0 all-to-all-done.mine_ref
  44.5 0.6 shard_map.39
  45.1 1.6 %collective-permute-start.9 = (bf16[4,128,512]{2,1,0:T(8,128)(2,1)S(1)}, bf16[4,128,512]{2,1,0:T(8,128)(2,1)S(1)}, u32[]{:S(2)}, u32[]{:S(2)}) collective-permute-start(bf16[4,128,512]{2,1,0:T(8,128)(2,1)S(1)} %get-tuple-element.33.refs_4_), channel_id=1, source_target_pairs={{0,2},{2,0},{4,6},{6,4},{8,10},{10,8},{12,14},{14,12},{1,3},{3,1},... | collective-permute-start | bytes 1572872 | tf_op jit(solution)/shard_map/ppermute | solution.py:219
  46.7 4.7 %collective-permute-start.10 = (bf16[4,128,512]{2,1,0:T(8,128)(2,1)S(1)}, bf16[4,128,512]{2,1,0:T(8,128)(2,1)S(1)}, u32[]{:S(2)}, u32[]{:S(2)}) collective-permute-start(bf16[4,128,512]{2,1,0:T(8,128)(2,1)S(1)} %get-tuple-element.34.refs_5_), channel_id=1, source_target_pairs={{0,14},{2,4},{4,2},{6,8},{8,6},{10,12},{12,10},{14,0},{1,15},{3,5}... | collective-permute-start | bytes 1572872 | tf_op jit(solution)/shard_map/ppermute | solution.py:219
  51.4 0.0 collective-permute-start.11
  51.4 1.1 %collective-permute-start.12 = (bf16[2,128,512]{2,1,0:T(8,128)(2,1)}, bf16[2,128,512]{2,1,0:T(8,128)(2,1)S(1)}, u32[]{:S(2)}, u32[]{:S(2)}) collective-permute-start(bf16[2,128,512]{2,1,0:T(8,128)(2,1)} %copy-done.8), channel_id=1, source_target_pairs={{0,192},{64,128},{128,64},{192,0},{1,193},{65,129},{129,65},{193,1... | collective-permute-start | bytes 786440 | tf_op jit(solution)/shard_map/ppermute | solution.py:213
  52.4 0.0 collective-permute-done.5.refs_0_
  52.4 3.1 %collective-permute-start.13 = (bf16[2,128,512]{2,1,0:T(8,128)(2,1)}, bf16[2,128,512]{2,1,0:T(8,128)(2,1)S(1)}, u32[]{:S(2)}, u32[]{:S(2)}) collective-permute-start(bf16[2,128,512]{2,1,0:T(8,128)(2,1)} %copy-done.7), channel_id=1, source_target_pairs={{0,32},{32,0},{1,33},{33,1},{2,34},{34,2},{3,35},{35,3},{4,36},{36... | collective-permute-start | bytes 786440 | tf_op jit(solution)/shard_map/ppermute | solution.py:213
  55.6 1.8 %shard_map.38 = (f32[512,512]{1,0:T(8,128)S(1)}, bf16[512,1536]{1,0:T(8,128)(2,1)S(1)}) custom-call(s32[1,3]{1,0:T(1,128)S(1)} %add_bitcast_fusion.place_ref, bf16[16,128,512]{2,1,0:T(8,128)(2,1)S(1)} %all-to-all-done.mine_ref, bf16[3,512,256]{2,1,0:T(8,128)(2,1)S(1)} %pad_maximum_fusion.refs_0_, bf16[3,512,256]{2,1,0:T(8,128)(2,1)S(1)} %copy-done.2, ...), custom_call_target="tpu_custom_call" | custom-call | tf_op jit(solution)/shard_map/pallas_call | solution.py:113
  57.4 0.4 collective-permute-done.11.refs_10_
  57.7 5.3 %collective-permute-start.6 = (bf16[1,512,256]{2,1,0:T(8,128)(2,1)S(1)}, bf16[1,512,256]{2,1,0:T(8,128)(2,1)S(1)}, u32[]{:S(2)}, u32[]{:S(2)}) collective-permute-start(bf16[1,512,256]{2,1,0:T(8,128)(2,1)S(1)} %collective-permute-done.5.refs_0_), channel_id=1, source_target_pairs={{0,33},{1,32},{32,1},{33,0},{2,35},{3,34},{34,3},{35,2},{4,37},{5,... | collective-permute-start | bytes 786440 | tf_op jit(solution)/shard_map/ppermute | solution.py:213
  63.0 0.0 collective-permute-done.12.refs_11_
  63.0 0.0 collective-permute-done.13.refs_12_
  63.0 0.0 collective-permute-done.9.refs_6_
  63.0 0.0 collective-permute-done.10.refs_7_
  63.1 0.1 pad_maximum_fusion.1
  63.2 2.0 %collective-permute-start.14 = (bf16[4,128,512]{2,1,0:T(8,128)(2,1)S(1)}, bf16[4,128,512]{2,1,0:T(8,128)(2,1)S(1)}, u32[]{:S(2)}, u32[]{:S(2)}) collective-permute-start(bf16[4,128,512]{2,1,0:T(8,128)(2,1)S(1)} %pad_maximum_fusion.1), channel_id=1, source_target_pairs={{0,16},{16,0},{1,17},{17,1},{2,18},{18,2},{3,19},{19,3},{4,20},{20... | collective-permute-start | bytes 1572872 | tf_op jit(solution)/shard_map/ppermute | solution.py:213
  65.2 0.1 collective-permute-start.7
  65.3 2.7 %collective-permute-done.6.refs_1_ = bf16[1,512,256]{2,1,0:T(8,128)(2,1)S(1)} collective-permute-done((bf16[1,512,256]{2,1,0:T(8,128)(2,1)S(1)}, bf16[1,512,256]{2,1,0:T(8,128)(2,1)S(1)}, u32[]{:S(2)}, u32[]{:S(2)}) %collective-permute-start.6) | collective-permute-done | bytes 262176 | tf_op jit(solution)/shard_map/ppermute | solution.py:213
  68.0 2.3 %collective-permute-start.8 = (bf16[1,512,256]{2,1,0:T(8,128)(2,1)S(1)}, bf16[1,512,256]{2,1,0:T(8,128)(2,1)S(1)}, u32[]{:S(2)}, u32[]{:S(2)}) collective-permute-start(bf16[1,512,256]{2,1,0:T(8,128)(2,1)S(1)} %collective-permute-done.6.refs_1_), channel_id=1, source_target_pairs={{0,16},{16,0},{1,17},{17,1},{2,18},{18,2},{3,19},{19,3},{4,20},{20... | collective-permute-start | bytes 786440 | tf_op jit(solution)/shard_map/ppermute | solution.py:213
  70.3 1.2 %collective-permute-done.8.refs_3_ = bf16[1,512,256]{2,1,0:T(8,128)(2,1)S(1)} collective-permute-done((bf16[1,512,256]{2,1,0:T(8,128)(2,1)S(1)}, bf16[1,512,256]{2,1,0:T(8,128)(2,1)S(1)}, u32[]{:S(2)}, u32[]{:S(2)}) %collective-permute-start.8) | collective-permute-done | bytes 262176 | tf_op jit(solution)/shard_map/ppermute | solution.py:213
  71.4 0.0 collective-permute-done.14.refs_8_
  71.4 5.8 %shard_map.40 = (f32[512,512]{1,0:T(8,128)S(1)}, f32[256,1,128]{2,1,0:T(1,128)S(1)}) custom-call(s32[1,3]{1,0:T(1,128)S(1)} %add_bitcast_fusion.place_ref, f32[512,512]{1,0:T(8,128)S(1)} %get-tuple-element.30.partial_ref, bf16[512,1536]{1,0:T(8,128)(2,1)S(1)} %get-tuple-element.31.rest_ref, bf16[1,512,256]{2,1,0:T(8,128)(2,1)S(1)} %collective-permute-done.5.refs_0_, ...), custom_call_target="tpu_custom_call" | custom-call | tf_op jit(solution)/shard_map/pallas_call | solution.py:177
  77.3 22.0 %all_to_all.10.sums_ref = f32[256,1,128]{2,1,0:T(1,128)S(1)} all-to-all(f32[256,1,128]{2,1,0:T(1,128)S(1)} %get-tuple-element.47), channel_id=1, replica_groups=mesh['x'=4,'yl'=2,'core'=2,'prec'=8,'pair'=2] {'x','yl','core','prec','p..., dimensions={0} | all-to-all | bytes 262144 | tf_op jit(solution)/shard_map/all_to_all | solution.py:254
  99.3 1.5 %shard_map.41 = f32[512,512]{1,0:T(8,128)} custom-call(f32[256,1,128]{2,1,0:T(1,128)S(1)} %all_to_all.10.sums_ref, f32[512,512]{1,0:T(8,128)S(1)} %get-tuple-element.48.update_ref), custom_call_target="tpu_custom_call" | custom-call | tf_op jit(solution)/shard_map/pallas_call | solution.py:200
  (19 shorter events, 0.1 us)
Async XLA Ops:
  1.1 9.6 %collective-permute-start.1 = (bf16[512,256]{1,0:T(8,128)(2,1)S(1)}, bf16[512,256]{1,0:T(8,128)(2,1)S(1)}, u32[]{:S(2)}, u32[]{:S(2)}) collective-permute-start(bf16[512,256]{1,0:T(8,128)(2,1)S(1)} %bitcast.11), channel_id=1, source_target_pairs={{0,192},{64,128},{128,64},{192,0},{1,193},{65,129},{129,65},{193,1... | collective-permute-start | bytes 786440 | tf_op jit(solution)/shard_map/ppermute | solution.py:213
  4.5 6.9 %collective-permute-start = (bf16[512,256]{1,0:T(8,128)(2,1)S(1)}, bf16[512,256]{1,0:T(8,128)(2,1)S(1)}, u32[]{:S(2)}, u32[]{:S(2)}) collective-permute-start(bf16[512,256]{1,0:T(8,128)(2,1)S(1)} %bitcast.12), channel_id=1, source_target_pairs={{0,64},{64,0},{128,192},{192,128},{1,65},{65,1},{129,193},{193,129... | collective-permute-start | bytes 786440 | tf_op jit(solution)/shard_map/ppermute | solution.py:213
  7.9 1.4 %copy-start = (bf16[16,128,512]{2,1,0:T(8,128)(2,1)}, bf16[16,128,512]{2,1,0:T(8,128)(2,1)S(1)}, u32[]{:S(2)}) copy-start(bf16[16,128,512]{2,1,0:T(8,128)(2,1)S(1)} %get-tuple-element.28) | copy-start | bytes 6291460
  9.3 0.7 copy-start.7
  10.0 0.7 copy-start.9
  10.7 0.7 copy-start.8
  11.4 33.1 %all-to-all-start = ((bf16[16,128,512]{2,1,0:T(8,128)(2,1)}), bf16[16,128,512]{2,1,0:T(8,128)(2,1)S(1)}, u32[]{:S(2)}, u32[]{:S(2)}) async-start(bf16[16,128,512]{2,1,0:T(8,128)(2,1)} %copy-done), calls=%async_computation | async-start | bytes 4194304 | tf_op jit(solution)/shard_map/all_to_all | solution.py:230
  17.3 20.2 %collective-permute-start.2 = (bf16[3,512,256]{2,1,0:T(8,128)(2,1)S(1)}, bf16[3,512,256]{2,1,0:T(8,128)(2,1)S(1)}, u32[]{:S(2)}, u32[]{:S(2)}) collective-permute-start(bf16[3,512,256]{2,1,0:T(8,128)(2,1)S(1)} %pad_maximum_fusion.refs_0_), channel_id=1, source_target_pairs={{0,33},{1,32},{32,1},{33,0},{2,35},{3,34},{34,3},{35,2},{4,37},{5,... | collective-permute-start | bytes 2359304 | tf_op jit(solution)/shard_map/ppermute | solution.py:213
  19.9 22.8 %collective-permute-start.3 = (bf16[3,512,256]{2,1,0:T(8,128)(2,1)S(1)}, bf16[3,512,256]{2,1,0:T(8,128)(2,1)S(1)}, u32[]{:S(2)}, u32[]{:S(2)}) collective-permute-start(bf16[3,512,256]{2,1,0:T(8,128)(2,1)S(1)} %pad_maximum_fusion.refs_0_), channel_id=1, source_target_pairs={{0,16},{16,0},{1,17},{17,1},{2,18},{18,2},{3,19},{19,3},{4,20},{20... | collective-permute-start | bytes 2359304 | tf_op jit(solution)/shard_map/ppermute | solution.py:213
  37.5 6.1 %collective-permute-start.4 = (bf16[3,512,256]{2,1,0:T(8,128)(2,1)S(1)}, bf16[3,512,256]{2,1,0:T(8,128)(2,1)S(1)}, u32[]{:S(2)}, u32[]{:S(2)}) collective-permute-start(bf16[3,512,256]{2,1,0:T(8,128)(2,1)S(1)} %collective-permute-done.2.refs_1_), channel_id=1, source_target_pairs={{0,16},{16,0},{1,17},{17,1},{2,18},{18,2},{3,19},{19,3},{4,20},{20... | collective-permute-start | bytes 2359304 | tf_op jit(solution)/shard_map/ppermute | solution.py:213
  38.5 0.9 copy-start.1
  40.1 12.3 %collective-permute-start.5 = (bf16[1,512,256]{2,1,0:T(8,128)(2,1)}, bf16[1,512,256]{2,1,0:T(8,128)(2,1)S(1)}, u32[]{:S(2)}, u32[]{:S(2)}) collective-permute-start(bf16[1,512,256]{2,1,0:T(8,128)(2,1)} %slice.15), channel_id=1, source_target_pairs={{0,192},{64,128},{128,64},{192,0},{1,193},{65,129},{129,65},{193,1... | collective-permute-start | bytes 786440 | tf_op jit(solution)/shard_map/ppermute | solution.py:213
  42.7 0.9 copy-start.3
  43.6 0.9 copy-start.5
  44.5 11.1 %copy-start.2 = (bf16[3,512,256]{2,1,0:T(8,128)(2,1)S(1)}, bf16[3,512,256]{2,1,0:T(8,128)(2,1)}, u32[]{:S(2)}) copy-start(bf16[3,512,256]{2,1,0:T(8,128)(2,1)} %copy-done.1) | copy-start | bytes 2359300
  44.5 11.1 %copy-start.4 = (bf16[3,512,256]{2,1,0:T(8,128)(2,1)S(1)}, bf16[3,512,256]{2,1,0:T(8,128)(2,1)}, u32[]{:S(2)}) copy-start(bf16[3,512,256]{2,1,0:T(8,128)(2,1)} %copy-done.3) | copy-start | bytes 2359300
  44.5 11.1 %copy-start.6 = (bf16[3,512,256]{2,1,0:T(8,128)(2,1)S(1)}, bf16[3,512,256]{2,1,0:T(8,128)(2,1)}, u32[]{:S(2)}) copy-start(bf16[3,512,256]{2,1,0:T(8,128)(2,1)} %copy-done.5) | copy-start | bytes 2359300
  45.1 17.9 %collective-permute-start.9 = (bf16[4,128,512]{2,1,0:T(8,128)(2,1)S(1)}, bf16[4,128,512]{2,1,0:T(8,128)(2,1)S(1)}, u32[]{:S(2)}, u32[]{:S(2)}) collective-permute-start(bf16[4,128,512]{2,1,0:T(8,128)(2,1)S(1)} %get-tuple-element.33.refs_4_), channel_id=1, source_target_pairs={{0,2},{2,0},{4,6},{6,4},{8,10},{10,8},{12,14},{14,12},{1,3},{3,1},... | collective-permute-start | bytes 1572872 | tf_op jit(solution)/shard_map/ppermute | solution.py:219
  46.7 16.4 %collective-permute-start.10 = (bf16[4,128,512]{2,1,0:T(8,128)(2,1)S(1)}, bf16[4,128,512]{2,1,0:T(8,128)(2,1)S(1)}, u32[]{:S(2)}, u32[]{:S(2)}) collective-permute-start(bf16[4,128,512]{2,1,0:T(8,128)(2,1)S(1)} %get-tuple-element.34.refs_5_), channel_id=1, source_target_pairs={{0,14},{2,4},{4,2},{6,8},{8,6},{10,12},{12,10},{14,0},{1,15},{3,5}... | collective-permute-start | bytes 1572872 | tf_op jit(solution)/shard_map/ppermute | solution.py:219
  51.4 6.4 %collective-permute-start.11 = (bf16[2,128,512]{2,1,0:T(8,128)(2,1)}, bf16[2,128,512]{2,1,0:T(8,128)(2,1)S(1)}, u32[]{:S(2)}, u32[]{:S(2)}) collective-permute-start(bf16[2,128,512]{2,1,0:T(8,128)(2,1)} %copy-done.9), channel_id=1, source_target_pairs={{0,64},{64,0},{128,192},{192,128},{1,65},{65,1},{129,193},{193,129... | collective-permute-start | bytes 786440 | tf_op jit(solution)/shard_map/ppermute | solution.py:213
  51.4 11.7 %collective-permute-start.12 = (bf16[2,128,512]{2,1,0:T(8,128)(2,1)}, bf16[2,128,512]{2,1,0:T(8,128)(2,1)S(1)}, u32[]{:S(2)}, u32[]{:S(2)}) collective-permute-start(bf16[2,128,512]{2,1,0:T(8,128)(2,1)} %copy-done.8), channel_id=1, source_target_pairs={{0,192},{64,128},{128,64},{192,0},{1,193},{65,129},{129,65},{193,1... | collective-permute-start | bytes 786440 | tf_op jit(solution)/shard_map/ppermute | solution.py:213
  52.4 10.6 %collective-permute-start.13 = (bf16[2,128,512]{2,1,0:T(8,128)(2,1)}, bf16[2,128,512]{2,1,0:T(8,128)(2,1)S(1)}, u32[]{:S(2)}, u32[]{:S(2)}) collective-permute-start(bf16[2,128,512]{2,1,0:T(8,128)(2,1)} %copy-done.7), channel_id=1, source_target_pairs={{0,32},{32,0},{1,33},{33,1},{2,34},{34,2},{3,35},{35,3},{4,36},{36... | collective-permute-start | bytes 786440 | tf_op jit(solution)/shard_map/ppermute | solution.py:213
  57.7 10.2 %collective-permute-start.6 = (bf16[1,512,256]{2,1,0:T(8,128)(2,1)S(1)}, bf16[1,512,256]{2,1,0:T(8,128)(2,1)S(1)}, u32[]{:S(2)}, u32[]{:S(2)}) collective-permute-start(bf16[1,512,256]{2,1,0:T(8,128)(2,1)S(1)} %collective-permute-done.5.refs_0_), channel_id=1, source_target_pairs={{0,33},{1,32},{32,1},{33,0},{2,35},{3,34},{34,3},{35,2},{4,37},{5,... | collective-permute-start | bytes 786440 | tf_op jit(solution)/shard_map/ppermute | solution.py:213
  63.2 8.3 %collective-permute-start.14 = (bf16[4,128,512]{2,1,0:T(8,128)(2,1)S(1)}, bf16[4,128,512]{2,1,0:T(8,128)(2,1)S(1)}, u32[]{:S(2)}, u32[]{:S(2)}) collective-permute-start(bf16[4,128,512]{2,1,0:T(8,128)(2,1)S(1)} %pad_maximum_fusion.1), channel_id=1, source_target_pairs={{0,16},{16,0},{1,17},{17,1},{2,18},{18,2},{3,19},{19,3},{4,20},{20... | collective-permute-start | bytes 1572872 | tf_op jit(solution)/shard_map/ppermute | solution.py:213
  65.2 5.1 %collective-permute-start.7 = (bf16[1,512,256]{2,1,0:T(8,128)(2,1)S(1)}, bf16[1,512,256]{2,1,0:T(8,128)(2,1)S(1)}, u32[]{:S(2)}, u32[]{:S(2)}) collective-permute-start(bf16[1,512,256]{2,1,0:T(8,128)(2,1)S(1)} %collective-permute-done.5.refs_0_), channel_id=1, source_target_pairs={{0,16},{16,0},{1,17},{17,1},{2,18},{18,2},{3,19},{19,3},{4,20},{20... | collective-permute-start | bytes 786440 | tf_op jit(solution)/shard_map/ppermute | solution.py:213
  68.0 3.5 %collective-permute-start.8 = (bf16[1,512,256]{2,1,0:T(8,128)(2,1)S(1)}, bf16[1,512,256]{2,1,0:T(8,128)(2,1)S(1)}, u32[]{:S(2)}, u32[]{:S(2)}) collective-permute-start(bf16[1,512,256]{2,1,0:T(8,128)(2,1)S(1)} %collective-permute-done.6.refs_1_), channel_id=1, source_target_pairs={{0,16},{16,0},{1,17},{17,1},{2,18},{18,2},{3,19},{19,3},{4,20},{20... | collective-permute-start | bytes 786440 | tf_op jit(solution)/shard_map/ppermute | solution.py:213

commit v6 on v5

--- a/solution.py
+++ b/solution.py
@@ -35,8 +35,11 @@
 
 def product(left, right, contract=ROWS_BY_COLUMNS):
     (left_high, left_low), (right_high, right_low) = left, right
-    return dot(left_high, right_high, contract) + (
-        dot(left_high, right_low, contract) + dot(left_low, right_high, contract)
+    axis = contract[0][1][0]
+    return dot(
+        jnp.concatenate([left_high, left_low, left_high], axis=1),
+        jnp.concatenate([right_high, right_high, right_low], axis=axis),
+        contract,
     )
 
 

time: 101 us -> 101 us (level)
  no operation moved by 1% of the time
where the time goes in v6:
time: 101 us
  starting transfers between devices  36.2 us (36%)
  blocking collectives  22 us (22%)
  waiting for transfers between devices  21.8 us (22%)
  Pallas kernels  12.2 us (12%)
  local copies, waits for them, and re-layouts  7.29 us (7%)
    ppermute x13, starting transfers between devices, swap(): return lax.ppermute(value, axes, [(i, i ^ bits) for i in range(size)])  24.1 us
    all_to_all x1, blocking collectives, per_device(): sums = lax.all_to_all(sums, EVERY, 0, 0, tiled=True)  22 us
    ppermute x13, waiting for transfers between devices, swap(): return lax.ppermute(value, axes, [(i, i ^ bits) for i in range(size)])  21.8 us
    unnamed x21, local copies, waits for them, and re-layouts  6.51 us
    ppermute x2, starting transfers between devices, swap_planes(): return lax.ppermute(value, 'prec', pairs)  6.23 us
    all_to_all x1, starting transfers between devices, per_device(): mine = lax.all_to_all(mine, DP, 0, 0, tiled=True)  5.87 us
    pallas_call x1, Pallas kernels, run_block(): pl.pallas_call(block_step, out_shape=(jax.ShapeDtypeStruct((BLK, BLK), jn...  5.63 us
    pallas_call x1, Pallas kernels, cut(): pl.pallas_call(cut_step, out_shape=[jax.ShapeDtypeStruct((shards, HALF, B...  2.69 us
  transfers between devices with their start and end apart: 16, of which 5 were waited for; matrix products, arithmetic and copies ran while one was open for 1% of the time, Pallas kernels for 5%

profile of v6, /device:TPU:1, one launch (start us, length us, event | category | flops | bytes accessed | tf_op | source)
XLA Modules:
  0.0 100.6 jit_solution(18076781610035755750)
XLA Ops:
  0.0 1.1 %copy.4 = bf16[256,512]{0,1:T(8,128)(2,1)S(1)} copy(bf16[256,512]{1,0:T(8,128)(2,1)} %param.3) | data formatting | bytes 524288 | tf_op args[0]
  1.1 3.4 %collective-permute-start.1 = (bf16[512,256]{1,0:T(8,128)(2,1)S(1)}, bf16[512,256]{1,0:T(8,128)(2,1)S(1)}, u32[]{:S(2)}, u32[]{:S(2)}) collective-permute-start(bf16[512,256]{1,0:T(8,128)(2,1)S(1)} %bitcast.11), channel_id=1, source_target_pairs={{0,192},{64,128},{128,64},{192,0},{1,193},{65,129},{129,65},{193,1... | collective-permute-start | bytes 786440 | tf_op jit(solution)/shard_map/ppermute | solution.py:216
  4.5 0.0 collective-permute-start
  5.1 0.1 add_bitcast_fusion.place_ref
  5.2 2.7 %shard_map.37 = (bf16[16,128,512]{2,1,0:T(8,128)(2,1)S(1)}, bf16[2,128,512]{2,1,0:T(8,128)(2,1)S(1)}, bf16[2,128,512]{2,1,0:T(8,128)(2,1)S(1)}, bf16[2,128,512]{2,1,0:T(8,128)(2,1)S(1)}, bf16[2,128,512]{2,1,0:T(8,128)(2,1)S(1)}) custom-call(s32[1,3]{1,0:T(1,128)S(1)} %add_bitcast_fusion.place_ref, bf16[256,8192]{1,0:T(8,128)(2,1)} %grads_ref.1), custom_call_target="tpu_custom_call" | custom-call | tf_op jit(solution)/shard_map/pallas_call | solution.py:71
  7.9 1.3 %copy-done = bf16[16,128,512]{2,1,0:T(8,128)(2,1)} copy-done((bf16[16,128,512]{2,1,0:T(8,128)(2,1)}, bf16[16,128,512]{2,1,0:T(8,128)(2,1)S(1)}, u32[]{:S(2)}) %copy-start) | copy-done | bytes 2097176
  9.3 0.7 copy-done.7
  10.0 0.7 copy-done.9
  10.7 0.0 collective-permute-done.1
  10.7 0.7 collective-permute-done
  11.3 0.1 pad_maximum_fusion.refs_0_
  11.4 5.9 %all-to-all-start = ((bf16[16,128,512]{2,1,0:T(8,128)(2,1)}), bf16[16,128,512]{2,1,0:T(8,128)(2,1)S(1)}, u32[]{:S(2)}, u32[]{:S(2)}) async-start(bf16[16,128,512]{2,1,0:T(8,128)(2,1)} %copy-done), calls=%async_computation | async-start | bytes 4194304 | tf_op jit(solution)/shard_map/all_to_all | solution.py:233
  17.3 2.6 %collective-permute-start.2 = (bf16[3,512,256]{2,1,0:T(8,128)(2,1)S(1)}, bf16[3,512,256]{2,1,0:T(8,128)(2,1)S(1)}, u32[]{:S(2)}, u32[]{:S(2)}) collective-permute-start(bf16[3,512,256]{2,1,0:T(8,128)(2,1)S(1)} %pad_maximum_fusion.refs_0_), channel_id=1, source_target_pairs={{0,33},{1,32},{32,1},{33,0},{2,35},{3,34},{34,3},{35,2},{4,37},{5,... | collective-permute-start | bytes 2359304 | tf_op jit(solution)/shard_map/ppermute | solution.py:216
  19.9 0.6 collective-permute-start.3
  20.6 16.9 %collective-permute-done.2.refs_1_ = bf16[3,512,256]{2,1,0:T(8,128)(2,1)S(1)} collective-permute-done((bf16[3,512,256]{2,1,0:T(8,128)(2,1)S(1)}, bf16[3,512,256]{2,1,0:T(8,128)(2,1)S(1)}, u32[]{:S(2)}, u32[]{:S(2)}) %collective-permute-start.2) | collective-permute-done | bytes 786464 | tf_op jit(solution)/shard_map/ppermute | solution.py:216
  37.5 1.0 collective-permute-start.4
  38.5 0.9 copy-done.1
  39.4 0.7 slice.15
  40.1 2.6 %collective-permute-start.5 = (bf16[1,512,256]{2,1,0:T(8,128)(2,1)}, bf16[1,512,256]{2,1,0:T(8,128)(2,1)S(1)}, u32[]{:S(2)}, u32[]{:S(2)}) collective-permute-start(bf16[1,512,256]{2,1,0:T(8,128)(2,1)} %slice.15), channel_id=1, source_target_pairs={{0,192},{64,128},{128,64},{192,0},{1,193},{65,129},{129,65},{193,1... | collective-permute-start | bytes 786440 | tf_op jit(solution)/shard_map/ppermute | solution.py:216
  42.7 0.0 collective-permute-done.3.refs_2_
  42.7 0.9 copy-done.3
  43.6 0.0 collective-permute-done.4.refs_3_
  43.6 0.9 copy-done.5
  44.5 0.0 all-to-all-done.mine_ref
  44.5 0.6 shard_map.39
  45.1 1.6 %collective-permute-start.9 = (bf16[4,128,512]{2,1,0:T(8,128)(2,1)S(1)}, bf16[4,128,512]{2,1,0:T(8,128)(2,1)S(1)}, u32[]{:S(2)}, u32[]{:S(2)}) collective-permute-start(bf16[4,128,512]{2,1,0:T(8,128)(2,1)S(1)} %get-tuple-element.33.refs_4_), channel_id=1, source_target_pairs={{0,2},{2,0},{4,6},{6,4},{8,10},{10,8},{12,14},{14,12},{1,3},{3,1},... | collective-permute-start | bytes 1572872 | tf_op jit(solution)/shard_map/ppermute | solution.py:222
  46.7 4.7 %collective-permute-start.10 = (bf16[4,128,512]{2,1,0:T(8,128)(2,1)S(1)}, bf16[4,128,512]{2,1,0:T(8,128)(2,1)S(1)}, u32[]{:S(2)}, u32[]{:S(2)}) collective-permute-start(bf16[4,128,512]{2,1,0:T(8,128)(2,1)S(1)} %get-tuple-element.34.refs_5_), channel_id=1, source_target_pairs={{0,14},{2,4},{4,2},{6,8},{8,6},{10,12},{12,10},{14,0},{1,15},{3,5}... | collective-permute-start | bytes 1572872 | tf_op jit(solution)/shard_map/ppermute | solution.py:222
  51.4 0.0 collective-permute-start.11
  51.4 1.1 %collective-permute-start.12 = (bf16[2,128,512]{2,1,0:T(8,128)(2,1)}, bf16[2,128,512]{2,1,0:T(8,128)(2,1)S(1)}, u32[]{:S(2)}, u32[]{:S(2)}) collective-permute-start(bf16[2,128,512]{2,1,0:T(8,128)(2,1)} %copy-done.8), channel_id=1, source_target_pairs={{0,192},{64,128},{128,64},{192,0},{1,193},{65,129},{129,65},{193,1... | collective-permute-start | bytes 786440 | tf_op jit(solution)/shard_map/ppermute | solution.py:216
  52.4 0.0 collective-permute-done.5.refs_0_
  52.4 3.1 %collective-permute-start.13 = (bf16[2,128,512]{2,1,0:T(8,128)(2,1)}, bf16[2,128,512]{2,1,0:T(8,128)(2,1)S(1)}, u32[]{:S(2)}, u32[]{:S(2)}) collective-permute-start(bf16[2,128,512]{2,1,0:T(8,128)(2,1)} %copy-done.7), channel_id=1, source_target_pairs={{0,32},{32,0},{1,33},{33,1},{2,34},{34,2},{3,35},{35,3},{4,36},{36... | collective-permute-start | bytes 786440 | tf_op jit(solution)/shard_map/ppermute | solution.py:216
  55.6 1.8 %shard_map.38 = (f32[512,512]{1,0:T(8,128)S(1)}, bf16[512,1536]{1,0:T(8,128)(2,1)S(1)}) custom-call(s32[1,3]{1,0:T(1,128)S(1)} %add_bitcast_fusion.place_ref, bf16[16,128,512]{2,1,0:T(8,128)(2,1)S(1)} %all-to-all-done.mine_ref, bf16[3,512,256]{2,1,0:T(8,128)(2,1)S(1)} %pad_maximum_fusion.refs_0_, bf16[3,512,256]{2,1,0:T(8,128)(2,1)S(1)} %copy-done.2, ...), custom_call_target="tpu_custom_call" | custom-call | tf_op jit(solution)/shard_map/pallas_call | solution.py:116
  57.4 0.4 collective-permute-done.11.refs_10_
  57.7 5.3 %collective-permute-start.6 = (bf16[1,512,256]{2,1,0:T(8,128)(2,1)S(1)}, bf16[1,512,256]{2,1,0:T(8,128)(2,1)S(1)}, u32[]{:S(2)}, u32[]{:S(2)}) collective-permute-start(bf16[1,512,256]{2,1,0:T(8,128)(2,1)S(1)} %collective-permute-done.5.refs_0_), channel_id=1, source_target_pairs={{0,33},{1,32},{32,1},{33,0},{2,35},{3,34},{34,3},{35,2},{4,37},{5,... | collective-permute-start | bytes 786440 | tf_op jit(solution)/shard_map/ppermute | solution.py:216
  63.0 0.0 collective-permute-done.12.refs_11_
  63.0 0.0 collective-permute-done.13.refs_12_
  63.0 0.0 collective-permute-done.9.refs_6_
  63.0 0.0 collective-permute-done.10.refs_7_
  63.1 0.1 pad_maximum_fusion.1
  63.2 2.0 %collective-permute-start.14 = (bf16[4,128,512]{2,1,0:T(8,128)(2,1)S(1)}, bf16[4,128,512]{2,1,0:T(8,128)(2,1)S(1)}, u32[]{:S(2)}, u32[]{:S(2)}) collective-permute-start(bf16[4,128,512]{2,1,0:T(8,128)(2,1)S(1)} %pad_maximum_fusion.1), channel_id=1, source_target_pairs={{0,16},{16,0},{1,17},{17,1},{2,18},{18,2},{3,19},{19,3},{4,20},{20... | collective-permute-start | bytes 1572872 | tf_op jit(solution)/shard_map/ppermute | solution.py:216
  65.2 0.1 collective-permute-start.7
  65.3 2.7 %collective-permute-done.6.refs_1_ = bf16[1,512,256]{2,1,0:T(8,128)(2,1)S(1)} collective-permute-done((bf16[1,512,256]{2,1,0:T(8,128)(2,1)S(1)}, bf16[1,512,256]{2,1,0:T(8,128)(2,1)S(1)}, u32[]{:S(2)}, u32[]{:S(2)}) %collective-permute-start.6) | collective-permute-done | bytes 262176 | tf_op jit(solution)/shard_map/ppermute | solution.py:216
  68.0 2.3 %collective-permute-start.8 = (bf16[1,512,256]{2,1,0:T(8,128)(2,1)S(1)}, bf16[1,512,256]{2,1,0:T(8,128)(2,1)S(1)}, u32[]{:S(2)}, u32[]{:S(2)}) collective-permute-start(bf16[1,512,256]{2,1,0:T(8,128)(2,1)S(1)} %collective-permute-done.6.refs_1_), channel_id=1, source_target_pairs={{0,16},{16,0},{1,17},{17,1},{2,18},{18,2},{3,19},{19,3},{4,20},{20... | collective-permute-start | bytes 786440 | tf_op jit(solution)/shard_map/ppermute | solution.py:216
  70.3 0.0 collective-permute-done.7.refs_2_
  70.3 1.2 %collective-permute-done.8.refs_3_ = bf16[1,512,256]{2,1,0:T(8,128)(2,1)S(1)} collective-permute-done((bf16[1,512,256]{2,1,0:T(8,128)(2,1)S(1)}, bf16[1,512,256]{2,1,0:T(8,128)(2,1)S(1)}, u32[]{:S(2)}, u32[]{:S(2)}) %collective-permute-start.8) | collective-permute-done | bytes 262176 | tf_op jit(solution)/shard_map/ppermute | solution.py:216
  71.4 5.6 %shard_map.40 = (f32[512,512]{1,0:T(8,128)S(1)}, f32[256,1,128]{2,1,0:T(1,128)S(1)}) custom-call(s32[1,3]{1,0:T(1,128)S(1)} %add_bitcast_fusion.place_ref, f32[512,512]{1,0:T(8,128)S(1)} %get-tuple-element.30.partial_ref, bf16[512,1536]{1,0:T(8,128)(2,1)S(1)} %get-tuple-element.31.rest_ref, bf16[1,512,256]{2,1,0:T(8,128)(2,1)S(1)} %collective-permute-done.5.refs_0_, ...), custom_call_target="tpu_custom_call" | custom-call | tf_op jit(solution)/shard_map/pallas_call | solution.py:180
  77.1 22.0 %all_to_all.10.sums_ref = f32[256,1,128]{2,1,0:T(1,128)S(1)} all-to-all(f32[256,1,128]{2,1,0:T(1,128)S(1)} %get-tuple-element.47), channel_id=1, replica_groups=mesh['x'=4,'yl'=2,'core'=2,'prec'=8,'pair'=2] {'x','yl','core','prec','p..., dimensions={0} | all-to-all | bytes 262144 | tf_op jit(solution)/shard_map/all_to_all | solution.py:257
  99.1 1.5 %shard_map.41 = f32[512,512]{1,0:T(8,128)} custom-call(f32[256,1,128]{2,1,0:T(1,128)S(1)} %all_to_all.10.sums_ref, f32[512,512]{1,0:T(8,128)S(1)} %get-tuple-element.48.update_ref), custom_call_target="tpu_custom_call" | custom-call | tf_op jit(solution)/shard_map/pallas_call | solution.py:203
  (19 shorter events, 0.1 us)
Async XLA Ops:
  1.1 9.6 %collective-permute-start.1 = (bf16[512,256]{1,0:T(8,128)(2,1)S(1)}, bf16[512,256]{1,0:T(8,128)(2,1)S(1)}, u32[]{:S(2)}, u32[]{:S(2)}) collective-permute-start(bf16[512,256]{1,0:T(8,128)(2,1)S(1)} %bitcast.11), channel_id=1, source_target_pairs={{0,192},{64,128},{128,64},{192,0},{1,193},{65,129},{129,65},{193,1... | collective-permute-start | bytes 786440 | tf_op jit(solution)/shard_map/ppermute | solution.py:216
  4.5 6.9 %collective-permute-start = (bf16[512,256]{1,0:T(8,128)(2,1)S(1)}, bf16[512,256]{1,0:T(8,128)(2,1)S(1)}, u32[]{:S(2)}, u32[]{:S(2)}) collective-permute-start(bf16[512,256]{1,0:T(8,128)(2,1)S(1)} %bitcast.12), channel_id=1, source_target_pairs={{0,64},{64,0},{128,192},{192,128},{1,65},{65,1},{129,193},{193,129... | collective-permute-start | bytes 786440 | tf_op jit(solution)/shard_map/ppermute | solution.py:216
  7.9 1.4 %copy-start = (bf16[16,128,512]{2,1,0:T(8,128)(2,1)}, bf16[16,128,512]{2,1,0:T(8,128)(2,1)S(1)}, u32[]{:S(2)}) copy-start(bf16[16,128,512]{2,1,0:T(8,128)(2,1)S(1)} %get-tuple-element.28) | copy-start | bytes 6291460
  9.3 0.7 copy-start.7
  10.0 0.7 copy-start.9
  10.7 0.7 copy-start.8
  11.4 33.1 %all-to-all-start = ((bf16[16,128,512]{2,1,0:T(8,128)(2,1)}), bf16[16,128,512]{2,1,0:T(8,128)(2,1)S(1)}, u32[]{:S(2)}, u32[]{:S(2)}) async-start(bf16[16,128,512]{2,1,0:T(8,128)(2,1)} %copy-done), calls=%async_computation | async-start | bytes 4194304 | tf_op jit(solution)/shard_map/all_to_all | solution.py:233
  17.3 20.2 %collective-permute-start.2 = (bf16[3,512,256]{2,1,0:T(8,128)(2,1)S(1)}, bf16[3,512,256]{2,1,0:T(8,128)(2,1)S(1)}, u32[]{:S(2)}, u32[]{:S(2)}) collective-permute-start(bf16[3,512,256]{2,1,0:T(8,128)(2,1)S(1)} %pad_maximum_fusion.refs_0_), channel_id=1, source_target_pairs={{0,33},{1,32},{32,1},{33,0},{2,35},{3,34},{34,3},{35,2},{4,37},{5,... | collective-permute-start | bytes 2359304 | tf_op jit(solution)/shard_map/ppermute | solution.py:216
  19.9 22.8 %collective-permute-start.3 = (bf16[3,512,256]{2,1,0:T(8,128)(2,1)S(1)}, bf16[3,512,256]{2,1,0:T(8,128)(2,1)S(1)}, u32[]{:S(2)}, u32[]{:S(2)}) collective-permute-start(bf16[3,512,256]{2,1,0:T(8,128)(2,1)S(1)} %pad_maximum_fusion.refs_0_), channel_id=1, source_target_pairs={{0,16},{16,0},{1,17},{17,1},{2,18},{18,2},{3,19},{19,3},{4,20},{20... | collective-permute-start | bytes 2359304 | tf_op jit(solution)/shard_map/ppermute | solution.py:216
  37.5 6.1 %collective-permute-start.4 = (bf16[3,512,256]{2,1,0:T(8,128)(2,1)S(1)}, bf16[3,512,256]{2,1,0:T(8,128)(2,1)S(1)}, u32[]{:S(2)}, u32[]{:S(2)}) collective-permute-start(bf16[3,512,256]{2,1,0:T(8,128)(2,1)S(1)} %collective-permute-done.2.refs_1_), channel_id=1, source_target_pairs={{0,16},{16,0},{1,17},{17,1},{2,18},{18,2},{3,19},{19,3},{4,20},{20... | collective-permute-start | bytes 2359304 | tf_op jit(solution)/shard_map/ppermute | solution.py:216
  38.5 0.9 copy-start.1
  40.1 12.3 %collective-permute-start.5 = (bf16[1,512,256]{2,1,0:T(8,128)(2,1)}, bf16[1,512,256]{2,1,0:T(8,128)(2,1)S(1)}, u32[]{:S(2)}, u32[]{:S(2)}) collective-permute-start(bf16[1,512,256]{2,1,0:T(8,128)(2,1)} %slice.15), channel_id=1, source_target_pairs={{0,192},{64,128},{128,64},{192,0},{1,193},{65,129},{129,65},{193,1... | collective-permute-start | bytes 786440 | tf_op jit(solution)/shard_map/ppermute | solution.py:216
  42.7 0.9 copy-start.3
  43.6 0.9 copy-start.5
  44.5 11.1 %copy-start.2 = (bf16[3,512,256]{2,1,0:T(8,128)(2,1)S(1)}, bf16[3,512,256]{2,1,0:T(8,128)(2,1)}, u32[]{:S(2)}) copy-start(bf16[3,512,256]{2,1,0:T(8,128)(2,1)} %copy-done.1) | copy-start | bytes 2359300
  44.5 11.1 %copy-start.4 = (bf16[3,512,256]{2,1,0:T(8,128)(2,1)S(1)}, bf16[3,512,256]{2,1,0:T(8,128)(2,1)}, u32[]{:S(2)}) copy-start(bf16[3,512,256]{2,1,0:T(8,128)(2,1)} %copy-done.3) | copy-start | bytes 2359300
  44.5 11.1 %copy-start.6 = (bf16[3,512,256]{2,1,0:T(8,128)(2,1)S(1)}, bf16[3,512,256]{2,1,0:T(8,128)(2,1)}, u32[]{:S(2)}) copy-start(bf16[3,512,256]{2,1,0:T(8,128)(2,1)} %copy-done.5) | copy-start | bytes 2359300
  45.1 17.9 %collective-permute-start.9 = (bf16[4,128,512]{2,1,0:T(8,128)(2,1)S(1)}, bf16[4,128,512]{2,1,0:T(8,128)(2,1)S(1)}, u32[]{:S(2)}, u32[]{:S(2)}) collective-permute-start(bf16[4,128,512]{2,1,0:T(8,128)(2,1)S(1)} %get-tuple-element.33.refs_4_), channel_id=1, source_target_pairs={{0,2},{2,0},{4,6},{6,4},{8,10},{10,8},{12,14},{14,12},{1,3},{3,1},... | collective-permute-start | bytes 1572872 | tf_op jit(solution)/shard_map/ppermute | solution.py:222
  46.7 16.4 %collective-permute-start.10 = (bf16[4,128,512]{2,1,0:T(8,128)(2,1)S(1)}, bf16[4,128,512]{2,1,0:T(8,128)(2,1)S(1)}, u32[]{:S(2)}, u32[]{:S(2)}) collective-permute-start(bf16[4,128,512]{2,1,0:T(8,128)(2,1)S(1)} %get-tuple-element.34.refs_5_), channel_id=1, source_target_pairs={{0,14},{2,4},{4,2},{6,8},{8,6},{10,12},{12,10},{14,0},{1,15},{3,5}... | collective-permute-start | bytes 1572872 | tf_op jit(solution)/shard_map/ppermute | solution.py:222
  51.4 6.4 %collective-permute-start.11 = (bf16[2,128,512]{2,1,0:T(8,128)(2,1)}, bf16[2,128,512]{2,1,0:T(8,128)(2,1)S(1)}, u32[]{:S(2)}, u32[]{:S(2)}) collective-permute-start(bf16[2,128,512]{2,1,0:T(8,128)(2,1)} %copy-done.9), channel_id=1, source_target_pairs={{0,64},{64,0},{128,192},{192,128},{1,65},{65,1},{129,193},{193,129... | collective-permute-start | bytes 786440 | tf_op jit(solution)/shard_map/ppermute | solution.py:216
  51.4 11.7 %collective-permute-start.12 = (bf16[2,128,512]{2,1,0:T(8,128)(2,1)}, bf16[2,128,512]{2,1,0:T(8,128)(2,1)S(1)}, u32[]{:S(2)}, u32[]{:S(2)}) collective-permute-start(bf16[2,128,512]{2,1,0:T(8,128)(2,1)} %copy-done.8), channel_id=1, source_target_pairs={{0,192},{64,128},{128,64},{192,0},{1,193},{65,129},{129,65},{193,1... | collective-permute-start | bytes 786440 | tf_op jit(solution)/shard_map/ppermute | solution.py:216
  52.4 10.6 %collective-permute-start.13 = (bf16[2,128,512]{2,1,0:T(8,128)(2,1)}, bf16[2,128,512]{2,1,0:T(8,128)(2,1)S(1)}, u32[]{:S(2)}, u32[]{:S(2)}) collective-permute-start(bf16[2,128,512]{2,1,0:T(8,128)(2,1)} %copy-done.7), channel_id=1, source_target_pairs={{0,32},{32,0},{1,33},{33,1},{2,34},{34,2},{3,35},{35,3},{4,36},{36... | collective-permute-start | bytes 786440 | tf_op jit(solution)/shard_map/ppermute | solution.py:216
  57.7 10.2 %collective-permute-start.6 = (bf16[1,512,256]{2,1,0:T(8,128)(2,1)S(1)}, bf16[1,512,256]{2,1,0:T(8,128)(2,1)S(1)}, u32[]{:S(2)}, u32[]{:S(2)}) collective-permute-start(bf16[1,512,256]{2,1,0:T(8,128)(2,1)S(1)} %collective-permute-done.5.refs_0_), channel_id=1, source_target_pairs={{0,33},{1,32},{32,1},{33,0},{2,35},{3,34},{34,3},{35,2},{4,37},{5,... | collective-permute-start | bytes 786440 | tf_op jit(solution)/shard_map/ppermute | solution.py:216
  63.2 8.3 %collective-permute-start.14 = (bf16[4,128,512]{2,1,0:T(8,128)(2,1)S(1)}, bf16[4,128,512]{2,1,0:T(8,128)(2,1)S(1)}, u32[]{:S(2)}, u32[]{:S(2)}) collective-permute-start(bf16[4,128,512]{2,1,0:T(8,128)(2,1)S(1)} %pad_maximum_fusion.1), channel_id=1, source_target_pairs={{0,16},{16,0},{1,17},{17,1},{2,18},{18,2},{3,19},{19,3},{4,20},{20... | collective-permute-start | bytes 1572872 | tf_op jit(solution)/shard_map/ppermute | solution.py:216
  65.2 5.1 %collective-permute-start.7 = (bf16[1,512,256]{2,1,0:T(8,128)(2,1)S(1)}, bf16[1,512,256]{2,1,0:T(8,128)(2,1)S(1)}, u32[]{:S(2)}, u32[]{:S(2)}) collective-permute-start(bf16[1,512,256]{2,1,0:T(8,128)(2,1)S(1)} %collective-permute-done.5.refs_0_), channel_id=1, source_target_pairs={{0,16},{16,0},{1,17},{17,1},{2,18},{18,2},{3,19},{19,3},{4,20},{20... | collective-permute-start | bytes 786440 | tf_op jit(solution)/shard_map/ppermute | solution.py:216
  68.0 3.5 %collective-permute-start.8 = (bf16[1,512,256]{2,1,0:T(8,128)(2,1)S(1)}, bf16[1,512,256]{2,1,0:T(8,128)(2,1)S(1)}, u32[]{:S(2)}, u32[]{:S(2)}) collective-permute-start(bf16[1,512,256]{2,1,0:T(8,128)(2,1)S(1)} %collective-permute-done.6.refs_1_), channel_id=1, source_target_pairs={{0,16},{16,0},{1,17},{17,1},{2,18},{18,2},{3,19},{19,3},{4,20},{20... | collective-permute-start | bytes 786440 | tf_op jit(solution)/shard_map/ppermute | solution.py:216
